TPU v7x, 32 devices: a whole 2x2x4 slice. The times are simulated.
32 devices in a mesh: groups: 1, dp: 16 (over z, y, x), mp: 2 (over core).
Axes of the slice: x: 2, y: 2, z: 4, core: 2. Of those that a mesh axis runs over, the one named last changes fastest.
Arguments:
- tokens: bfloat16 [6144, 8192], P(('groups', 'dp'), 'mp'), may hold values from -6 to 6
- cotangent: bfloat16 [6144, 8192], P(('groups', 'dp'), 'mp'), may hold values from -6 to 6
- lengths: int32 [16, 4], P(('groups', 'dp')), may hold values from 48 to 96, as said below
- up_first: bfloat16 [128, 4096], P('mp', 'dp'), may hold values from -0.75 to 0.75
- up_second: bfloat16 [128, 16384], P('mp', 'dp'), may hold values from -0.75 to 0.75
- down_first: bfloat16 [128, 16384], P('mp', 'dp'), may hold values from -0.375 to 0.375
- down_second: bfloat16 [128, 4096], P('mp', 'dp'), may hold values from -0.75 to 0.75
Outputs:
- input_grad: bfloat16 [6144, 8192], P(('groups', 'dp'), 'mp')
- grad_up_first: float32 [128, 4096], P(('groups', 'mp'), 'dp')
- grad_up_second: float32 [128, 16384], P(('groups', 'mp'), 'dp')
- grad_down_first: float32 [128, 16384], P(('groups', 'mp'), 'dp')
- grad_down_second: float32 [128, 4096], P(('groups', 'mp'), 'dp')
Inputs may be any that keep to these rules, and one draw needn't show every extreme that they name: `lengths`: every microbatch has one segment of exactly 96 tokens.
All inputs are finite; a program needn't handle non-finite values.
Results may differ from a plain program's by a relative error of at most 0.019.
Values may be sent and summed in bfloat16 or wider, within the bound.
A program may use at most 192 MiB of HBM per device.

v0:
```python
import jax
import jax.numpy as jnp
from jax import lax
from jax.sharding import PartitionSpec as P

P_SIZE = 64
Q = 256
SEG_MOST = 96


def smooth(values):
    return (
        0.5
        * values
        * (1.0 + jnp.tanh(0.7978845608028654 * (values + 0.044715 * values * values * values)))
    )


def token_scale(seg_lengths, count):
    ends = jnp.cumsum(seg_lengths)
    starts = ends - seg_lengths
    positions = jnp.arange(count, dtype=jnp.int32)[:, None]
    inside = (positions >= starts[None, :]) & (positions < ends[None, :])
    weights = SEG_MOST / seg_lengths.astype(jnp.float32)
    return jnp.sum(jnp.where(inside, weights[None, :], jnp.zeros_like(weights)[None, :]), axis=1)


def to_second(field, shares):
    row_count, inner, blocks = field.shape
    grouped = field.reshape(row_count, shares, inner // shares * blocks)
    moved = lax.all_to_all(grouped, "mp", split_axis=1, concat_axis=1, tiled=True)
    moved = moved.reshape(row_count, shares, inner // shares, blocks).transpose(0, 2, 1, 3)
    return moved.reshape(row_count, inner, blocks)


def to_first(field, shares):
    row_count, blocks, width = field.shape
    grouped = field.reshape(row_count, blocks // shares, shares, width).transpose(0, 2, 1, 3)
    grouped = grouped.reshape(row_count, shares, blocks // shares * width)
    moved = lax.all_to_all(grouped, "mp", split_axis=1, concat_axis=1, tiled=True)
    return moved.reshape(row_count, blocks, width)


def shards(tokens, cotangent, lengths, up_first, up_second, down_first, down_second):
    single_float = jnp.float32
    brain_float_half = jnp.bfloat16
    shares = lax.axis_size("mp")
    local_blocks = up_first.shape[0]
    row_count = tokens.shape[0]
    whole_one, whole_two, whole_three, whole_four = (
        lax.all_gather(up_first, "dp", axis=1, tiled=True),
        lax.all_gather(up_second, "dp", axis=1, tiled=True),
        lax.all_gather(down_first, "dp", axis=1, tiled=True),
        lax.all_gather(down_second, "dp", axis=1, tiled=True),
    )
    wone = whole_one.reshape(local_blocks, P_SIZE, P_SIZE)
    wtwo = whole_two.reshape(local_blocks, P_SIZE, Q)
    third_weight = whole_three.reshape(local_blocks, Q, P_SIZE)
    wfour = whole_four.reshape(local_blocks, P_SIZE, P_SIZE)
    blocked = tokens.reshape(row_count, local_blocks, P_SIZE)
    first = jnp.einsum("tmp,mpj->tjm", blocked, wone, preferred_element_type=single_float).astype(
        brain_float_half
    )
    mixed_in = to_second(first, shares)
    pre_sum = jnp.einsum("tkm,kmq->tkq", mixed_in, wtwo, preferred_element_type=single_float)
    pre = pre_sum.astype(brain_float_half)
    gelu_activation = smooth(pre_sum).astype(brain_float_half)
    narrow_rows = jnp.einsum(
        "gxa,xad->gxd", gelu_activation, third_weight, preferred_element_type=single_float
    ).astype(brain_float_half)
    mixed_out = to_first(narrow_rows, shares)
    scale = token_scale(lengths[0], row_count)
    out_grad = (
        (cotangent.astype(single_float) * scale[:, None])
        .astype(brain_float_half)
        .reshape(row_count, local_blocks, P_SIZE)
    )
    g_four = jnp.einsum(
        "tjm,tmq->mjq", mixed_out, out_grad, preferred_element_type=single_float
    ).reshape(local_blocks, P_SIZE * P_SIZE)
    d_mixed_out = jnp.einsum(
        "tmq,mjq->tjm", out_grad, wfour, preferred_element_type=single_float
    ).astype(brain_float_half)
    narrow_gradient = to_second(d_mixed_out, shares)
    third_factor_gradient = jnp.einsum(
        "aus,auf->usf", gelu_activation, narrow_gradient, preferred_element_type=single_float
    ).reshape(local_blocks, Q * P_SIZE)
    activation_gradient = jnp.einsum(
        "wez,ehz->weh", narrow_gradient, third_weight, preferred_element_type=single_float
    )
    unused, pullback = jax.vjp(smooth, pre.astype(single_float))
    d_pre = pullback(activation_gradient)[0].astype(brain_float_half)
    g_two = jnp.einsum(
        "tkm,tkq->kmq", mixed_in, d_pre, preferred_element_type=single_float
    ).reshape(local_blocks, P_SIZE * Q)
    d_mixed_in = jnp.einsum(
        "tkq,kmq->tkm", d_pre, wtwo, preferred_element_type=single_float
    ).astype(brain_float_half)
    d_first = to_first(d_mixed_in, shares)
    g_one = jnp.einsum(
        "tmp,tjm->mpj", blocked, d_first, preferred_element_type=single_float
    ).reshape(local_blocks, P_SIZE * P_SIZE)
    input_grad = jnp.einsum(
        "tjm,mpj->tmp", d_first, wone, preferred_element_type=single_float
    ).astype(brain_float_half)
    input_grad = input_grad.reshape(row_count, local_blocks * P_SIZE)
    g_one, g_two, third_factor_gradient, g_four = (
        lax.psum_scatter(g_one.astype(jnp.bfloat16), "dp", scatter_dimension=1, tiled=True).astype(
            jnp.float32
        ),
        lax.psum_scatter(g_two.astype(jnp.bfloat16), "dp", scatter_dimension=1, tiled=True).astype(
            jnp.float32
        ),
        lax.psum_scatter(
            third_factor_gradient.astype(jnp.bfloat16), "dp", scatter_dimension=1, tiled=True
        ).astype(jnp.float32),
        lax.psum_scatter(g_four.astype(jnp.bfloat16), "dp", scatter_dimension=1, tiled=True).astype(
            jnp.float32
        ),
    )
    return (input_grad, g_one, g_two, third_factor_gradient, g_four)


def solution(mesh):
    in_specs = (
        P(("groups", "dp"), "mp"),
        P(("groups", "dp"), "mp"),
        P(("groups", "dp"), None),
        P("mp", "dp"),
        P("mp", "dp"),
        P("mp", "dp"),
        P("mp", "dp"),
    )
    out_specs = (
        P(("groups", "dp"), "mp"),
        P(("groups", "mp"), "dp"),
        P(("groups", "mp"), "dp"),
        P(("groups", "mp"), "dp"),
        P(("groups", "mp"), "dp"),
    )
    return jax.shard_map(shards, mesh=mesh, in_specs=in_specs, out_specs=out_specs, check_vma=False)
```

profile of v0, /device:TPU:0, one launch (start us, length us, event | category | flops | bytes accessed | tf_op | source)
XLA Modules:
  0.0 536.1 jit_solution(8373104087525022171)
XLA Ops:
  7.9 0.7 all-gather.5.cloned.1.call-update
  8.6 46.0 %all_gather.12 = bf16[64,4096]{1,0:T(8,128)(2,1)S(1)} all-gather(bf16[64,256]{1,0:T(8,128)(2,1)} %param.10), channel_id=1, replica_groups=mesh['groups'=1,'dp'=16,'mp'=2] {'dp'}, dimensions={1}, use_global_device_ids=true | all-gather | bytes 557056 | tf_op jit(solution)/shard_map/all_gather | solution.py:51
  54.7 2.1 reshape.86
  56.8 3.5 copy.35
  60.3 3.0 convert_bitcast_fusion.1
  63.4 3.6 copy.37
  66.9 4.1 all-to-all-start
  71.0 41.8 %all_gather.14 = bf16[64,4096]{1,0:T(8,128)(2,1)} all-gather(bf16[64,256]{1,0:T(8,128)(2,1)S(1)} %copy-done.8), channel_id=1, replica_groups=mesh['groups'=1,'dp'=16,'mp'=2] {'dp'}, dimensions={1}, use_global_device_ids=true | all-gather | bytes 557056 | tf_op jit(solution)/shard_map/all_gather | solution.py:54
  112.9 2.8 reshape.95
  115.6 4.6 copy.39
  120.5 2.9 multiply_convert_fusion
  123.4 1.0 convert_bitcast_fusion
  125.0 3.5 copy.40
  128.6 5.2 all-to-all-start.1
  134.0 2.2 copy.38
  136.2 1.4 all-to-all-done.1
  137.5 2.3 copy.41
  139.9 3.4 copy.55
  143.3 6.5 %reshape.99 = bf16[64,256,64]{2,1,0:T(8,128)(2,1)} reshape(bf16[64,16384]{1,0:T(8,128)(2,1)} %all-gather.5.cloned.1.call-done) | data formatting | bytes 4194304 | tf_op jit(solution)/shard_map/reshape | solution.py:58
  149.8 14.0 %fusion.37 = f32[64,384,256]{2,1,0:T(8,128)} fusion(bf16[384,64,64]{0,2,1:T(8,128)(2,1)S(1)} %bitcast.83, bf16[64,256,64]{2,1,0:T(8,128)(2,1)} %reshape.99), kind=kOutput, calls=%fused_computation.53 | convolution fusion | flops 805306368 | bytes 30408704 | tf_op jit(solution)/shard_map/wez,ehz->weh/dot_general | solution.py:88
  163.8 29.0 %fusion.9 = (bf16[384,64,256]{2,0,1:T(8,128)(2,1)S(1)}, bf16[384,64,256]{2,0,1:T(8,128)(2,1)}) fusion(f32[64,384,256]{2,1,0:T(8,128)} %fusion.37, bf16[384,64,64]{0,2,1:T(8,128)(2,1)} %bitcast.86, bf16[64,64,256]{2,1,0:T(8,128)(2,1)} %bitcast.102), kind=kOutput, calls=%fused_computation.18 | convolution fusion | flops 1025507328 | bytes 55574528 | tf_op jit(solution)/shard_map/tkm,kmq->tkq/dot_general | solution.py:65
  192.8 10.9 %convolution_convert_fusion = bf16[64,384,64]{1,2,0:T(8,128)(2,1)} fusion(bf16[384,64,256]{2,0,1:T(8,128)(2,1)S(1)} %get-tuple-element.20, bf16[64,256,64]{2,1,0:T(8,128)(2,1)} %reshape.99), kind=kOutput, calls=%fused_computation.39 | convolution fusion | flops 806879232 | bytes 17825792 | tf_op jit(solution)/shard_map/gxa,xad->gxd/dot_general | solution.py:68
  203.7 2.3 copy.49
  206.0 6.5 %all_to_all.20 = bf16[384,2,2048]{0,2,1:T(8,128)(2,1)S(1)} all-to-all(bf16[384,2,2048]{0,2,1:T(8,128)(2,1)S(1)} %bitcast.99), channel_id=1, replica_groups=mesh['groups'=1,'dp'=16,'mp'=2] {'mp'}, dimensions={1} | all-to-all | bytes 6291456 | tf_op jit(solution)/shard_map/all_to_all | solution.py:40
  212.5 3.2 fusion.29
  215.7 2.7 convert_element_type.119
  218.5 10.8 %convolution_convert_fusion.1 = bf16[64,384,64]{1,2,0:T(8,128)(2,1)} fusion(bf16[384,64,256]{2,0,1:T(8,128)(2,1)} %get-tuple-element.21, bf16[64,64,256]{2,1,0:T(8,128)(2,1)} %bitcast.103), kind=kOutput, calls=%fused_computation.40 | convolution fusion | flops 806879232 | bytes 17825792 | tf_op jit(solution)/shard_map/tkq,kmq->tkm/dot_general | solution.py:96
  229.4 2.3 copy.43
  231.7 6.8 %all_to_all.21 = bf16[384,2,2048]{0,2,1:T(8,128)(2,1)S(1)} all-to-all(bf16[384,2,2048]{0,2,1:T(8,128)(2,1)S(1)} %bitcast.100), channel_id=1, replica_groups=mesh['groups'=1,'dp'=16,'mp'=2] {'mp'}, dimensions={1} | all-to-all | bytes 6291456 | tf_op jit(solution)/shard_map/all_to_all | solution.py:40
  238.4 1.7 copy-done.5
  240.1 3.2 fusion.32
  243.3 2.3 copy.46
  245.6 2.7 convert_element_type.107
  248.4 7.9 %convolution_convert_fusion.3 = bf16[64,64,256]{2,1,0:T(8,128)(2,1)S(1)} fusion(bf16[384,64,64]{0,2,1:T(8,128)(2,1)} %bitcast.87, bf16[384,64,256]{2,0,1:T(8,128)(2,1)} %get-tuple-element.21), kind=kOutput, calls=%fused_computation.42 | convolution fusion | flops 806354944 | bytes 17825792 | tf_op jit(solution)/shard_map/tkm,tkq->kmq/dot_general | solution.py:93
  256.3 2.6 copy.56
  259.0 8.3 %convolution_convert_fusion.2 = bf16[64,256,64]{1,2,0:T(8,128)(2,1)} fusion(bf16[384,64,64]{0,2,1:T(8,128)(2,1)S(1)} %bitcast.84, bf16[384,64,256]{2,0,1:T(8,128)(2,1)} %copy-done), kind=kOutput, calls=%fused_computation.41 | convolution fusion | flops 806354944 | bytes 17825792 | tf_op jit(solution)/shard_map/aus,auf->usf/dot_general | solution.py:85
  267.3 5.1 copy.47
  272.3 6.1 %convert_element_type.114 = bf16[64,16384]{1,0:T(8,128)(2,1)} reshape(bf16[64,256,64]{2,1,0:T(8,128)(2,1)} %copy.47) | data formatting | bytes 4194304 | tf_op jit(solution)/shard_map/convert_element_type | solution.py:115
  278.5 5.7 %fusion.23 = bf16[64,384,64]{1,2,0:T(8,128)(2,1)} fusion(bf16[64,64,64]{2,1,0:T(8,128)(2,1)} %reshape.86, bf16[384,64,64]{0,2,1:T(8,128)(2,1)S(1)} %bitcast.94), kind=kOutput, calls=%fused_computation.38 | convolution fusion | flops 202899456 | bytes 6815744 | tf_op jit(solution)/shard_map/tjm,mpj->tmp/dot_general | solution.py:103
  284.2 4.6 copy.51
  288.8 4.0 reduce-scatter.11.cloned.1.call-done
  292.8 1.4 convert_element_type.120
  294.2 73.8 %reduce-scatter.5.cloned.1.call-done = bf16[64,256]{1,0:T(8,128)(2,1)} async-done(((bf16[64,4096]{1,0:T(8,128)(2,1)}), bf16[64,256]{1,0:T(8,128)(2,1)}) %reduce-scatter.5.cloned.1.call-update) | async-done | bytes 32784 | tf_op jit(solution)/shard_map/reduce_scatter | solution.py:108
  368.0 1.4 convert_element_type.108
  369.4 78.0 %reduce-scatter.7.cloned.1.call-done = bf16[64,1024]{1,0:T(8,128)(2,1)} async-done(((bf16[64,16384]{1,0:T(8,128)(2,1)}), bf16[64,1024]{1,0:T(8,128)(2,1)}) %reduce-scatter.7.cloned.1.call-update) | async-done | bytes 131088 | tf_op jit(solution)/shard_map/reduce_scatter | solution.py:111
  447.4 1.6 convert_element_type.111
  449.0 78.1 %reduce-scatter.9.cloned.1.call-done = bf16[64,1024]{1,0:T(8,128)(2,1)} async-done(((bf16[64,16384]{1,0:T(8,128)(2,1)}), bf16[64,1024]{1,0:T(8,128)(2,1)}) %reduce-scatter.9.cloned.1.call-update) | async-done | bytes 131088 | tf_op jit(solution)/shard_map/reduce_scatter | solution.py:114
  527.1 1.6 convert_element_type.115
  (37 shorter events, 2.1 us)
Async XLA Ops:
  7.2 132.7 %all-gather.3.cloned.1.call-start = ((), (), s32[]{:S(2)}) async-start(), calls=%async_computation.8 | async-start | bytes 2228224 | tf_op jit(solution)/shard_map/all_gather | solution.py:52
  7.9 135.4 %all-gather.5.cloned.1.call-start = ((), (), s32[]{:S(2)}) async-start(), calls=%async_computation.9 | async-start | bytes 2228224 | tf_op jit(solution)/shard_map/all_gather | solution.py:53
  60.3 3.1 copy-start.1
  66.9 4.1 copy-start.8
  66.9 61.6 %all-to-all-start = ((bf16[384,2,2048]{0,2,1:T(8,128)(2,1)}), bf16[384,2,2048]{0,2,1:T(8,128)(2,1)S(1)}, u32[]{:S(2)}, u32[]{:S(2)}) async-start(bf16[384,2,2048]{0,2,1:T(8,128)(2,1)} %bitcast.97), calls=%async_computation | async-start | bytes 6291456 | tf_op jit(solution)/shard_map/all_to_all | solution.py:31
  115.6 4.6 copy-start.9
  120.5 2.9 copy-start.7
  123.4 1.6 copy-start.3
  128.6 9.0 %all-to-all-start.1 = ((bf16[384,2,2048]{0,2,1:T(8,128)(2,1)}), bf16[384,2,2048]{0,2,1:T(8,128)(2,1)}, u32[]{:S(2)}, u32[]{:S(2)}) async-start(bf16[384,2,2048]{0,2,1:T(8,128)(2,1)} %bitcast.98), calls=%async_computation.1 | async-start | bytes 6291456 | tf_op jit(solution)/shard_map/all_to_all | solution.py:31
  133.8 159.0 %reduce-scatter.11.cloned.1.call-start = ((), (), s32[]{:S(2)}) async-start(), calls=%async_computation.13 | async-start | bytes 557056 | tf_op jit(solution)/shard_map/reduce_scatter | solution.py:117
  192.8 10.9 %copy-start = (bf16[384,64,256]{2,0,1:T(8,128)(2,1)}, bf16[384,64,256]{2,0,1:T(8,128)(2,1)S(1)}, u32[]{:S(2)}) copy-start(bf16[384,64,256]{2,0,1:T(8,128)(2,1)S(1)} %get-tuple-element.20) | copy-start | bytes 37748740
  206.0 6.5 %copy-start.4 = (bf16[384,4096]{0,1:T(8,128)(2,1)S(1)}, bf16[384,4096]{0,1:T(8,128)(2,1)}, u32[]{:S(2)}) copy-start(bf16[384,4096]{0,1:T(8,128)(2,1)} %copy-done.3) | copy-start | bytes 9437188
  218.5 149.5 %reduce-scatter.5.cloned.1.call-start = ((), (), s32[]{:S(2)}) async-start(), calls=%async_computation.10 | async-start | bytes 557056 | tf_op jit(solution)/shard_map/reduce_scatter | solution.py:108
  231.7 8.4 %copy-start.2 = (bf16[384,4096]{0,1:T(8,128)(2,1)S(1)}, bf16[384,4096]{0,1:T(8,128)(2,1)}, u32[]{:S(2)}) copy-start(bf16[384,4096]{0,1:T(8,128)(2,1)} %copy-done.1) | copy-start | bytes 9437188
  238.4 1.7 copy-start.5
  248.3 199.1 %reduce-scatter.7.cloned.1.call-start = ((), (), s32[]{:S(2)}) async-start(), calls=%async_computation.11 | async-start | bytes 2228224 | tf_op jit(solution)/shard_map/reduce_scatter | solution.py:111
  258.9 268.2 %reduce-scatter.9.cloned.1.call-start = ((), (), s32[]{:S(2)}) async-start(), calls=%async_computation.12 | async-start | bytes 2228224 | tf_op jit(solution)/shard_map/reduce_scatter | solution.py:114
  272.3 6.2 %copy-start.6 = (bf16[384,2,2048]{0,2,1:T(8,128)(2,1)S(1)}, bf16[384,2,2048]{0,2,1:T(8,128)(2,1)}, u32[]{:S(2)}) copy-start(bf16[384,2,2048]{0,2,1:T(8,128)(2,1)} %copy-done.5) | copy-start | bytes 9437188
Sparse Core Ops, SparseCore 0:
  10.7 65.2 all-gather.2
  78.8 60.0 all-gather.4
  218.6 74.1 reduce-scatter.10
  295.0 72.9 reduce-scatter.4
  370.1 77.2 reduce-scatter.6
  449.5 77.5 reduce-scatter.8
where the time goes:
time: 544 us; the launch traced here: 536 us
  waiting for transfers between devices  237 us (44%)
  blocking collectives  101 us (19%)
  matrix products  97 us (18%)
  local copies, waits for them, and re-layouts  67.5 us (12%)
  between operations  14.8 us (3%)
  starting transfers between devices  9.71 us (2%)
  other arithmetic  9.18 us (2%)
    reduce_scatter x1, waiting for transfers between devices, shards(): lax.psum_scatter(third_factor_gradient.astype(jnp.bfloat16), 'dp', scatte...  78.1 us
    reduce_scatter x1, waiting for transfers between devices, shards(): lax.psum_scatter(g_two.astype(jnp.bfloat16), 'dp', scatter_dimension=1, t...  78 us
    reduce_scatter x1, waiting for transfers between devices, shards(): lax.psum_scatter(g_one.astype(jnp.bfloat16), 'dp', scatter_dimension=1, t...  73.8 us
    all_gather x1, blocking collectives, shards(): lax.all_gather(up_first, 'dp', axis=1, tiled=True)  46 us
    all_gather x1, blocking collectives, shards(): lax.all_gather(down_second, 'dp', axis=1, tiled=True)  41.8 us
    dot_general x1, matrix products, shards(): jnp.einsum('tkm,kmq->tkq', mixed_in, wtwo, preferred_element_type=single_...  29 us
    unnamed x25, local copies, waits for them, and re-layouts  21.1 us
    dot_general x1, matrix products, shards(): jnp.einsum('wez,ehz->weh', narrow_gradient, third_weight, preferred_eleme...  14 us
  transfers between devices with their start and end apart: 8, of which 5 were waited for; matrix products, arithmetic and copies ran while one was open for 19% of the time, Pallas kernels for 0%

commit v1 on v0

--- a/solution.py
+++ b/solution.py
@@ -17,7 +17,10 @@
 
 
 def token_scale(seg_lengths, count):
-    ends = jnp.cumsum(seg_lengths)
+    order = jnp.arange(seg_lengths.shape[0], dtype=jnp.int32)
+    ends = jnp.sum(
+        jnp.where(order[None, :] <= order[:, None], seg_lengths[None, :], 0), axis=1
+    )
     starts = ends - seg_lengths
     positions = jnp.arange(count, dtype=jnp.int32)[:, None]
     inside = (positions >= starts[None, :]) & (positions < ends[None, :])

time: 544 us -> 544 us (level)
  no operation moved by 1% of the time
where the time goes in v1:
time: 544 us; the launch traced here: 536 us
  waiting for transfers between devices  236 us (43%)
  blocking collectives  101 us (19%)
  matrix products  97 us (18%)
  local copies, waits for them, and re-layouts  67.5 us (12%)
  between operations  14.8 us (3%)
  starting transfers between devices  9.71 us (2%)
  other arithmetic  9.12 us (2%)
    reduce_scatter x1, waiting for transfers between devices, shards(): lax.psum_scatter(third_factor_gradient.astype(jnp.bfloat16), 'dp', scatte...  78.1 us
    reduce_scatter x1, waiting for transfers between devices, shards(): lax.psum_scatter(g_two.astype(jnp.bfloat16), 'dp', scatter_dimension=1, t...  77.8 us
    reduce_scatter x1, waiting for transfers between devices, shards(): lax.psum_scatter(g_one.astype(jnp.bfloat16), 'dp', scatter_dimension=1, t...  73.7 us
    all_gather x1, blocking collectives, shards(): lax.all_gather(up_first, 'dp', axis=1, tiled=True)  46 us
    all_gather x1, blocking collectives, shards(): lax.all_gather(down_second, 'dp', axis=1, tiled=True)  41.8 us
    dot_general x1, matrix products, shards(): jnp.einsum('tkm,kmq->tkq', mixed_in, wtwo, preferred_element_type=single_...  29 us
    unnamed x25, local copies, waits for them, and re-layouts  21.1 us
    dot_general x1, matrix products, shards(): jnp.einsum('wez,ehz->weh', narrow_gradient, third_weight, preferred_eleme...  14 us
  transfers between devices with their start and end apart: 8, of which 5 were waited for; matrix products, arithmetic and copies ran while one was open for 19% of the time, Pallas kernels for 0%

profile of v1, /device:TPU:0, one launch (start us, length us, event | category | flops | bytes accessed | tf_op | source)
XLA Modules:
  0.0 535.8 jit_solution(2806740261412086625)
XLA Ops:
  7.9 0.7 all-gather.5.cloned.1.call-update
  8.6 46.0 %all_gather.12 = bf16[64,4096]{1,0:T(8,128)(2,1)S(1)} all-gather(bf16[64,256]{1,0:T(8,128)(2,1)} %param.10), channel_id=1, replica_groups=mesh['groups'=1,'dp'=16,'mp'=2] {'dp'}, dimensions={1}, use_global_device_ids=true | all-gather | bytes 557056 | tf_op jit(solution)/shard_map/all_gather | solution.py:54
  54.7 2.1 reshape.78
  56.8 3.5 copy.35
  60.3 3.0 convert_bitcast_fusion.1
  63.4 3.6 copy.37
  66.9 4.1 all-to-all-start
  71.0 41.8 %all_gather.14 = bf16[64,4096]{1,0:T(8,128)(2,1)} all-gather(bf16[64,256]{1,0:T(8,128)(2,1)S(1)} %copy-done.8), channel_id=1, replica_groups=mesh['groups'=1,'dp'=16,'mp'=2] {'dp'}, dimensions={1}, use_global_device_ids=true | all-gather | bytes 557056 | tf_op jit(solution)/shard_map/all_gather | solution.py:57
  112.9 2.8 reshape.85
  115.6 4.6 copy.39
  120.5 2.9 multiply_convert_fusion
  123.4 1.0 convert_bitcast_fusion
  125.0 3.5 copy.40
  128.5 5.2 all-to-all-start.1
  133.9 2.2 copy.38
  136.1 1.4 all-to-all-done.1
  137.5 2.3 copy.41
  139.8 3.4 copy.55
  143.3 6.5 %reshape.89 = bf16[64,256,64]{2,1,0:T(8,128)(2,1)} reshape(bf16[64,16384]{1,0:T(8,128)(2,1)} %all-gather.5.cloned.1.call-done) | data formatting | bytes 4194304 | tf_op jit(solution)/shard_map/reshape | solution.py:61
  149.8 14.0 %fusion.37 = f32[64,384,256]{2,1,0:T(8,128)} fusion(bf16[384,64,64]{0,2,1:T(8,128)(2,1)S(1)} %bitcast.82, bf16[64,256,64]{2,1,0:T(8,128)(2,1)} %reshape.89), kind=kOutput, calls=%fused_computation.55 | convolution fusion | flops 805306368 | bytes 30408704 | tf_op jit(solution)/shard_map/wez,ehz->weh/dot_general | solution.py:91
  163.7 29.0 %fusion.9 = (bf16[384,64,256]{2,0,1:T(8,128)(2,1)S(1)}, bf16[384,64,256]{2,0,1:T(8,128)(2,1)}) fusion(f32[64,384,256]{2,1,0:T(8,128)} %fusion.37, bf16[384,64,64]{0,2,1:T(8,128)(2,1)} %bitcast.85, bf16[64,64,256]{2,1,0:T(8,128)(2,1)} %bitcast.101), kind=kOutput, calls=%fused_computation.18 | convolution fusion | flops 1025507328 | bytes 55574528 | tf_op jit(solution)/shard_map/tkm,kmq->tkq/dot_general | solution.py:68
  192.7 10.9 %convolution_convert_fusion = bf16[64,384,64]{1,2,0:T(8,128)(2,1)} fusion(bf16[384,64,256]{2,0,1:T(8,128)(2,1)S(1)} %get-tuple-element.20, bf16[64,256,64]{2,1,0:T(8,128)(2,1)} %reshape.89), kind=kOutput, calls=%fused_computation.39 | convolution fusion | flops 806879232 | bytes 17825792 | tf_op jit(solution)/shard_map/gxa,xad->gxd/dot_general | solution.py:71
  203.7 2.3 copy.49
  206.0 6.5 %all_to_all.20 = bf16[384,2,2048]{0,2,1:T(8,128)(2,1)S(1)} all-to-all(bf16[384,2,2048]{0,2,1:T(8,128)(2,1)S(1)} %bitcast.98), channel_id=1, replica_groups=mesh['groups'=1,'dp'=16,'mp'=2] {'mp'}, dimensions={1} | all-to-all | bytes 6291456 | tf_op jit(solution)/shard_map/all_to_all | solution.py:43
  212.5 3.2 fusion.29
  215.7 2.7 convert_element_type.119
  218.5 10.8 %convolution_convert_fusion.1 = bf16[64,384,64]{1,2,0:T(8,128)(2,1)} fusion(bf16[384,64,256]{2,0,1:T(8,128)(2,1)} %get-tuple-element.21, bf16[64,64,256]{2,1,0:T(8,128)(2,1)} %bitcast.102), kind=kOutput, calls=%fused_computation.40 | convolution fusion | flops 806879232 | bytes 17825792 | tf_op jit(solution)/shard_map/tkq,kmq->tkm/dot_general | solution.py:99
  229.3 2.3 copy.43
  231.6 6.8 %all_to_all.21 = bf16[384,2,2048]{0,2,1:T(8,128)(2,1)S(1)} all-to-all(bf16[384,2,2048]{0,2,1:T(8,128)(2,1)S(1)} %bitcast.99), channel_id=1, replica_groups=mesh['groups'=1,'dp'=16,'mp'=2] {'mp'}, dimensions={1} | all-to-all | bytes 6291456 | tf_op jit(solution)/shard_map/all_to_all | solution.py:43
  238.4 1.7 copy-done.5
  240.0 3.2 fusion.32
  243.3 2.3 copy.46
  245.5 2.7 convert_element_type.107
  248.3 7.9 %convolution_convert_fusion.3 = bf16[64,64,256]{2,1,0:T(8,128)(2,1)S(1)} fusion(bf16[384,64,64]{0,2,1:T(8,128)(2,1)} %bitcast.86, bf16[384,64,256]{2,0,1:T(8,128)(2,1)} %get-tuple-element.21), kind=kOutput, calls=%fused_computation.42 | convolution fusion | flops 806354944 | bytes 17825792 | tf_op jit(solution)/shard_map/tkm,tkq->kmq/dot_general | solution.py:96
  256.3 2.6 copy.56
  258.9 8.3 %convolution_convert_fusion.2 = bf16[64,256,64]{1,2,0:T(8,128)(2,1)} fusion(bf16[384,64,64]{0,2,1:T(8,128)(2,1)S(1)} %bitcast.83, bf16[384,64,256]{2,0,1:T(8,128)(2,1)} %copy-done), kind=kOutput, calls=%fused_computation.41 | convolution fusion | flops 806354944 | bytes 17825792 | tf_op jit(solution)/shard_map/aus,auf->usf/dot_general | solution.py:88
  267.2 5.1 copy.47
  272.3 6.1 %convert_element_type.114 = bf16[64,16384]{1,0:T(8,128)(2,1)} reshape(bf16[64,256,64]{2,1,0:T(8,128)(2,1)} %copy.47) | data formatting | bytes 4194304 | tf_op jit(solution)/shard_map/convert_element_type | solution.py:118
  278.4 5.7 %fusion.23 = bf16[64,384,64]{1,2,0:T(8,128)(2,1)} fusion(bf16[64,64,64]{2,1,0:T(8,128)(2,1)} %reshape.78, bf16[384,64,64]{0,2,1:T(8,128)(2,1)S(1)} %bitcast.93), kind=kOutput, calls=%fused_computation.38 | convolution fusion | flops 202899456 | bytes 6815744 | tf_op jit(solution)/shard_map/tjm,mpj->tmp/dot_general | solution.py:106
  284.1 4.6 copy.51
  288.8 4.0 reduce-scatter.11.cloned.1.call-done
  292.7 1.4 convert_element_type.120
  294.1 73.7 %reduce-scatter.5.cloned.1.call-done = bf16[64,256]{1,0:T(8,128)(2,1)} async-done(((bf16[64,4096]{1,0:T(8,128)(2,1)}), bf16[64,256]{1,0:T(8,128)(2,1)}) %reduce-scatter.5.cloned.1.call-update) | async-done | bytes 32784 | tf_op jit(solution)/shard_map/reduce_scatter | solution.py:111
  367.8 1.4 convert_element_type.108
  369.2 77.8 %reduce-scatter.7.cloned.1.call-done = bf16[64,1024]{1,0:T(8,128)(2,1)} async-done(((bf16[64,16384]{1,0:T(8,128)(2,1)}), bf16[64,1024]{1,0:T(8,128)(2,1)}) %reduce-scatter.7.cloned.1.call-update) | async-done | bytes 131088 | tf_op jit(solution)/shard_map/reduce_scatter | solution.py:114
  447.0 1.6 convert_element_type.111
  448.7 78.1 %reduce-scatter.9.cloned.1.call-done = bf16[64,1024]{1,0:T(8,128)(2,1)} async-done(((bf16[64,16384]{1,0:T(8,128)(2,1)}), bf16[64,1024]{1,0:T(8,128)(2,1)}) %reduce-scatter.9.cloned.1.call-update) | async-done | bytes 131088 | tf_op jit(solution)/shard_map/reduce_scatter | solution.py:117
  526.8 1.6 convert_element_type.115
  (37 shorter events, 2.1 us)
Async XLA Ops:
  7.2 132.6 %all-gather.3.cloned.1.call-start = ((), (), s32[]{:S(2)}) async-start(), calls=%async_computation.8 | async-start | bytes 2228224 | tf_op jit(solution)/shard_map/all_gather | solution.py:55
  7.9 135.4 %all-gather.5.cloned.1.call-start = ((), (), s32[]{:S(2)}) async-start(), calls=%async_computation.9 | async-start | bytes 2228224 | tf_op jit(solution)/shard_map/all_gather | solution.py:56
  60.3 3.1 copy-start.1
  66.9 4.1 copy-start.8
  66.9 61.6 %all-to-all-start = ((bf16[384,2,2048]{0,2,1:T(8,128)(2,1)}), bf16[384,2,2048]{0,2,1:T(8,128)(2,1)S(1)}, u32[]{:S(2)}, u32[]{:S(2)}) async-start(bf16[384,2,2048]{0,2,1:T(8,128)(2,1)} %bitcast.96), calls=%async_computation | async-start | bytes 6291456 | tf_op jit(solution)/shard_map/all_to_all | solution.py:34
  115.6 4.6 copy-start.9
  120.5 2.9 copy-start.7
  123.4 1.6 copy-start.3
  128.5 9.0 %all-to-all-start.1 = ((bf16[384,2,2048]{0,2,1:T(8,128)(2,1)}), bf16[384,2,2048]{0,2,1:T(8,128)(2,1)}, u32[]{:S(2)}, u32[]{:S(2)}) async-start(bf16[384,2,2048]{0,2,1:T(8,128)(2,1)} %bitcast.97), calls=%async_computation.1 | async-start | bytes 6291456 | tf_op jit(solution)/shard_map/all_to_all | solution.py:34
  133.7 159.0 %reduce-scatter.11.cloned.1.call-start = ((), (), s32[]{:S(2)}) async-start(), calls=%async_computation.13 | async-start | bytes 557056 | tf_op jit(solution)/shard_map/reduce_scatter | solution.py:120
  192.7 10.9 %copy-start = (bf16[384,64,256]{2,0,1:T(8,128)(2,1)}, bf16[384,64,256]{2,0,1:T(8,128)(2,1)S(1)}, u32[]{:S(2)}) copy-start(bf16[384,64,256]{2,0,1:T(8,128)(2,1)S(1)} %get-tuple-element.20) | copy-start | bytes 37748740
  205.9 6.5 %copy-start.4 = (bf16[384,4096]{0,1:T(8,128)(2,1)S(1)}, bf16[384,4096]{0,1:T(8,128)(2,1)}, u32[]{:S(2)}) copy-start(bf16[384,4096]{0,1:T(8,128)(2,1)} %copy-done.3) | copy-start | bytes 9437188
  218.4 149.4 %reduce-scatter.5.cloned.1.call-start = ((), (), s32[]{:S(2)}) async-start(), calls=%async_computation.10 | async-start | bytes 557056 | tf_op jit(solution)/shard_map/reduce_scatter | solution.py:111
  231.6 8.4 %copy-start.2 = (bf16[384,4096]{0,1:T(8,128)(2,1)S(1)}, bf16[384,4096]{0,1:T(8,128)(2,1)}, u32[]{:S(2)}) copy-start(bf16[384,4096]{0,1:T(8,128)(2,1)} %copy-done.1) | copy-start | bytes 9437188
  238.4 1.7 copy-start.5
  248.3 198.8 %reduce-scatter.7.cloned.1.call-start = ((), (), s32[]{:S(2)}) async-start(), calls=%async_computation.11 | async-start | bytes 2228224 | tf_op jit(solution)/shard_map/reduce_scatter | solution.py:114
  258.9 267.9 %reduce-scatter.9.cloned.1.call-start = ((), (), s32[]{:S(2)}) async-start(), calls=%async_computation.12 | async-start | bytes 2228224 | tf_op jit(solution)/shard_map/reduce_scatter | solution.py:117
  272.3 6.2 %copy-start.6 = (bf16[384,2,2048]{0,2,1:T(8,128)(2,1)S(1)}, bf16[384,2,2048]{0,2,1:T(8,128)(2,1)}, u32[]{:S(2)}) copy-start(bf16[384,2,2048]{0,2,1:T(8,128)(2,1)} %copy-done.5) | copy-start | bytes 9437188
Sparse Core Ops, SparseCore 0:
  10.7 65.2 all-gather.2
  78.8 60.0 all-gather.4
  218.5 74.1 reduce-scatter.10
  294.9 72.8 reduce-scatter.4
  370.0 77.0 reduce-scatter.6
  449.2 77.5 reduce-scatter.8

commit v2 on v1

--- a/solution.py
+++ b/solution.py
@@ -50,12 +50,18 @@
     shares = lax.axis_size("mp")
     local_blocks = up_first.shape[0]
     row_count = tokens.shape[0]
-    whole_one, whole_two, whole_three, whole_four = (
-        lax.all_gather(up_first, "dp", axis=1, tiled=True),
-        lax.all_gather(up_second, "dp", axis=1, tiled=True),
-        lax.all_gather(down_first, "dp", axis=1, tiled=True),
-        lax.all_gather(down_second, "dp", axis=1, tiled=True),
-    )
+    parts = lax.axis_size("dp")
+
+    def gathered(left, right):
+        width = left.shape[1]
+        whole = lax.all_gather(jnp.concatenate([left, right], axis=1), "dp", axis=0)
+        return tuple(
+            piece.transpose(1, 0, 2).reshape(local_blocks, -1)
+            for piece in (whole[:, :, :width], whole[:, :, width:])
+        )
+
+    whole_one, whole_four = gathered(up_first, down_second)
+    whole_two, whole_three = gathered(up_second, down_first)
     wone = whole_one.reshape(local_blocks, P_SIZE, P_SIZE)
     wtwo = whole_two.reshape(local_blocks, P_SIZE, Q)
     third_weight = whole_three.reshape(local_blocks, Q, P_SIZE)
@@ -107,20 +113,18 @@
         "tjm,mpj->tmp", d_first, wone, preferred_element_type=single_float
     ).astype(brain_float_half)
     input_grad = input_grad.reshape(row_count, local_blocks * P_SIZE)
-    g_one, g_two, third_factor_gradient, g_four = (
-        lax.psum_scatter(g_one.astype(jnp.bfloat16), "dp", scatter_dimension=1, tiled=True).astype(
-            jnp.float32
-        ),
-        lax.psum_scatter(g_two.astype(jnp.bfloat16), "dp", scatter_dimension=1, tiled=True).astype(
-            jnp.float32
-        ),
-        lax.psum_scatter(
-            third_factor_gradient.astype(jnp.bfloat16), "dp", scatter_dimension=1, tiled=True
-        ).astype(jnp.float32),
-        lax.psum_scatter(g_four.astype(jnp.bfloat16), "dp", scatter_dimension=1, tiled=True).astype(
-            jnp.float32
-        ),
-    )
+    pieces = [
+        piece.astype(brain_float_half).reshape(local_blocks, parts, -1).transpose(1, 0, 2)
+        for piece in (g_one, g_two, third_factor_gradient, g_four)
+    ]
+    summed = lax.psum_scatter(
+        jnp.concatenate(pieces, axis=2), "dp", scatter_dimension=0, tiled=False
+    ).astype(single_float)
+    cuts, at = [], 0
+    for piece in pieces:
+        cuts.append(summed[:, at : at + piece.shape[2]])
+        at += piece.shape[2]
+    g_one, g_two, third_factor_gradient, g_four = cuts
     return (input_grad, g_one, g_two, third_factor_gradient, g_four)
 
 

time: 544 us -> 436 us (0.80)
  blocking collectives: 101 us -> 27.3 us
  waiting for transfers between devices: 236 us -> 197 us
  local copies, waits for them, and re-layouts: 67.5 us -> 82.2 us
  starting transfers between devices: 9.71 us -> 0.12 us
    reduce_scatter x4 -> x1, waiting for transfers between devices: 234 us -> 104 us  [shards(): lax.psum_scatter(jnp.concatenate(pieces, axis=2), 'dp', scatter_dimension...]
    all_gather x2, waiting for transfers between devices: 0.02 us -> 92.9 us  [gathered(): whole = lax.all_gather(jnp.concatenate([left, right], axis=1), 'dp', axis=0)]
    all_gather x2 -> x0, blocking collectives: 87.8 us -> none  [the longest x1 46 us: shards(): lax.all_gather(up_first, 'dp', axis=1, tiled=True)]
    another operation x0 -> x4, local copies, waits for them, and re-layouts: none -> 15.4 us  [the longest x1 6.37 us: shards(): third_weight = whole_three.reshape(local_blocks, Q, P_SIZE)]
    all_to_all x0 -> x2, blocking collectives: none -> 12.7 us  [to_second(): lax.all_to_all(grouped, 'mp', split_axis=1, concat_axis=1, tiled=True)]
    reshape x3 -> x0, local copies, waits for them, and re-layouts: 11.4 us -> none  [the longest x1 6.51 us: shards(): third_weight = whole_three.reshape(local_blocks, Q, P_SIZE)]
    all_to_all x2 -> x0, starting transfers between devices: 9.3 us -> none  [to_second(): lax.all_to_all(grouped, 'mp', split_axis=1, concat_axis=1, tiled=True)]
    slice x0 -> x4, local copies, waits for them, and re-layouts: none -> 6.9 us  [the longest x2 5.42 us: gathered(): whole[:, :, width:]]
  transfers between devices with their start and end apart: 8 -> 3, of which waited for: 5 -> 3; matrix products, arithmetic and copies ran while one was open for 19% -> 10% of each run, Pallas kernels for 0% -> 0%
where the time goes in v2:
time: 436 us; the launch traced here: 427 us
  waiting for transfers between devices  197 us (45%)
  matrix products  94.4 us (22%)
  local copies, waits for them, and re-layouts  82.2 us (19%)
  blocking collectives  27.3 us (6%)
  between operations  14.3 us (3%)
  other arithmetic  11.9 us (3%)
    reduce_scatter x1, waiting for transfers between devices, shards(): lax.psum_scatter(jnp.concatenate(pieces, axis=2), 'dp', scatter_dimension...  104 us
    all_gather x2, waiting for transfers between devices, gathered(): whole = lax.all_gather(jnp.concatenate([left, right], axis=1), 'dp', axis=0)  92.9 us
    dot_general x1, matrix products, shards(): jnp.einsum('tkm,kmq->tkq', mixed_in, wtwo, preferred_element_type=single_...  28.7 us
    convert_element_type x6, local copies, waits for them, and re-layouts, shards(): piece.astype(brain_float_half).reshape(local_blocks, parts, -1)  23.2 us
    unnamed x25, local copies, waits for them, and re-layouts  21.2 us
    all_to_all x2, blocking collectives, to_first(): lax.all_to_all(grouped, 'mp', split_axis=1, concat_axis=1, tiled=True)  14.6 us
    dot_general x1, matrix products, shards(): jnp.einsum('wez,ehz->weh', narrow_gradient, third_weight, preferred_eleme...  14.1 us
    all_to_all x2, blocking collectives, to_second(): lax.all_to_all(grouped, 'mp', split_axis=1, concat_axis=1, tiled=True)  12.7 us
  transfers between devices with their start and end apart: 3, of which 3 were waited for; matrix products, arithmetic and copies ran while one was open for 10% of the time, Pallas kernels for 0%

profile of v2, /device:TPU:0, one launch (start us, length us, event | category | flops | bytes accessed | tf_op | source)
XLA Modules:
  0.0 427.0 jit_solution(12771774151656850666)
XLA Ops:
  7.2 1.4 pad_maximum_fusion.2
  8.7 1.7 pad_maximum_fusion.1
  10.5 3.4 copy.79
  13.9 5.4 %copy.85 = bf16[384,4096]{0,1:T(8,128)(2,1)} copy(bf16[384,4096]{1,0:T(8,128)(2,1)} %param.8) | data formatting | bytes 6291456 | tf_op args[1]
  19.6 4.2 multiply_convert_fusion
  23.7 45.6 %all-gather.5.cloned.1.call-done = bf16[1024,512]{1,0:T(8,128)(2,1)} async-done(((bf16[64,512]{1,0:T(8,128)(2,1)}), bf16[1024,512]{1,0:T(8,128)(2,1)}) %all-gather.5.cloned.1.call-update) | async-done | bytes 1048592 | tf_op jit(solution)/shard_map/all_gather | solution.py:57
  69.4 1.3 fusion.38
  70.6 1.6 copy_bitcast_fusion.2
  72.2 2.3 reshape_reshape.15
  74.6 2.4 reshape_reshape.12
  76.9 2.2 convert_bitcast_fusion.1
  79.2 1.9 copy.81
  81.0 6.3 %all_to_all.20 = bf16[384,2,2048]{0,2,1:T(8,128)(2,1)S(1)} all-to-all(bf16[384,2,2048]{0,2,1:T(8,128)(2,1)S(1)} %bitcast.109), channel_id=1, replica_groups=mesh['groups'=1,'dp'=16,'mp'=2] {'mp'}, dimensions={1} | all-to-all | bytes 6291456 | tf_op jit(solution)/shard_map/all_to_all | solution.py:34
  87.3 2.1 copy.82
  89.4 0.9 copy-done.4
  90.6 1.0 convert_bitcast_fusion
  91.6 1.9 copy.86
  93.4 6.4 %all_to_all.21 = bf16[384,2,2048]{0,2,1:T(8,128)(2,1)S(1)} all-to-all(bf16[384,2,2048]{0,2,1:T(8,128)(2,1)S(1)} %bitcast.111), channel_id=1, replica_groups=mesh['groups'=1,'dp'=16,'mp'=2] {'mp'}, dimensions={1} | all-to-all | bytes 6291456 | tf_op jit(solution)/shard_map/all_to_all | solution.py:34
  100.3 47.3 %all-gather.7.cloned.1.call-done = bf16[1024,2048]{1,0:T(8,128)(2,1)} async-done(((bf16[64,2048]{1,0:T(8,128)(2,1)}), bf16[1024,2048]{1,0:T(8,128)(2,1)}) %all-gather.7.cloned.1.call-update) | async-done | bytes 4194320 | tf_op jit(solution)/shard_map/all_gather | solution.py:57
  147.6 4.2 fusion.37
  151.8 2.5 copy.132
  154.3 6.4 %reshape_reshape.14 = bf16[64,256,64]{2,1,0:T(8,128)(2,1)} reshape(bf16[64,16,1024]{2,1,0:T(8,128)(2,1)} %bitcast.118) | data formatting | bytes 4194304 | tf_op jit(solution)/shard_map/reshape;reshape | solution.py:67
  160.6 4.1 copy.133
  164.7 4.3 %reshape_reshape.13 = bf16[64,64,256]{2,1,0:T(8,128)(2,1)} reshape(bf16[64,16,1024]{2,1,0:T(8,128)(2,1)} %bitcast.119) | data formatting | bytes 4194304 | tf_op jit(solution)/shard_map/reshape;reshape | solution.py:66
  169.1 14.1 %fusion.41 = f32[64,256,384]{2,1,0:T(8,128)} fusion(bf16[64,256,64]{2,1,0:T(8,128)(2,1)} %reshape_reshape.14, bf16[384,64,64]{0,2,1:T(8,128)(2,1)S(1)} %bitcast.97), kind=kOutput, calls=%fused_computation.67 | convolution fusion | flops 805306368 | bytes 30408704 | tf_op jit(solution)/shard_map/wez,ehz->weh/dot_general | solution.py:97
  183.1 28.7 %fusion.9 = (bf16[384,64,256]{0,2,1:T(8,128)(2,1)}, bf16[384,64,256]{0,2,1:T(8,128)(2,1)}) fusion(f32[64,256,384]{2,1,0:T(8,128)} %fusion.41, bf16[64,64,256]{2,1,0:T(8,128)(2,1)S(1)} %copy-done.1, bf16[384,64,64]{0,2,1:T(8,128)(2,1)S(1)} %bitcast.115), kind=kOutput, calls=%fused_computation.18 | convolution fusion | flops 1025507328 | bytes 55574528 | tf_op jit(solution)/shard_map/tkm,kmq->tkq/dot_general | solution.py:74
  211.9 8.1 %convolution_convert_fusion = bf16[64,64,384]{2,1,0:T(8,128)(2,1)} fusion(bf16[64,256,64]{2,1,0:T(8,128)(2,1)S(1)} %copy-done, bf16[384,64,256]{0,2,1:T(8,128)(2,1)} %get-tuple-element.25), kind=kOutput, calls=%fused_computation.40 | convolution fusion | flops 806879232 | bytes 17825792 | tf_op jit(solution)/shard_map/gxa,xad->gxd/dot_general | solution.py:77
  220.0 10.0 %convolution_convert_fusion.2 = bf16[64,256,64]{1,2,0:T(8,128)(2,1)} fusion(bf16[384,64,256]{0,2,1:T(8,128)(2,1)} %get-tuple-element.25, bf16[384,64,64]{0,2,1:T(8,128)(2,1)S(1)} %bitcast.98), kind=kOutput, calls=%fused_computation.44 | convolution fusion | flops 806354944 | bytes 17825792 | tf_op jit(solution)/shard_map/aus,auf->usf/dot_general | solution.py:94
  230.0 10.9 %convolution_convert_fusion.3 = bf16[64,64,256]{2,1,0:T(8,128)(2,1)} fusion(bf16[384,64,64]{0,2,1:T(8,128)(2,1)} %bitcast.114, bf16[384,64,256]{0,2,1:T(8,128)(2,1)} %get-tuple-element.26), kind=kOutput, calls=%fused_computation.45 | convolution fusion | flops 806354944 | bytes 17825792 | tf_op jit(solution)/shard_map/tkm,tkq->kmq/dot_general | solution.py:102
  240.9 7.2 %convolution_convert_fusion.1 = bf16[64,64,384]{2,1,0:T(8,128)(2,1)S(1)} fusion(bf16[64,64,256]{2,1,0:T(8,128)(2,1)} %reshape_reshape.13, bf16[384,64,256]{0,2,1:T(8,128)(2,1)} %get-tuple-element.26), kind=kOutput, calls=%fused_computation.41 | convolution fusion | flops 806879232 | bytes 17825792 | tf_op jit(solution)/shard_map/tkq,kmq->tkm/dot_general | solution.py:105
  248.1 2.0 copy.99
  250.1 4.4 %convert_element_type.107 = bf16[64,16,1024]{2,1,0:T(8,128)(2,1)} reshape(bf16[64,64,256]{2,1,0:T(8,128)(2,1)} %convolution_convert_fusion.3) | data formatting | bytes 4194304 | tf_op jit(solution)/shard_map/convert_element_type | solution.py:117
  254.5 7.8 %all_to_all.22 = bf16[384,2,2048]{0,2,1:T(8,128)(2,1)S(1)} all-to-all(bf16[384,2,2048]{0,2,1:T(8,128)(2,1)} %bitcast.108), channel_id=1, replica_groups=mesh['groups'=1,'dp'=16,'mp'=2] {'mp'}, dimensions={1} | all-to-all | bytes 6291456 | tf_op jit(solution)/shard_map/all_to_all | solution.py:43
  262.3 3.2 fusion.29
  265.5 2.6 convert_element_type.114
  268.5 6.8 %all_to_all.23 = bf16[384,2,2048]{0,2,1:T(8,128)(2,1)S(1)} all-to-all(bf16[384,2,2048]{0,2,1:T(8,128)(2,1)S(1)} %bitcast.113), channel_id=1, replica_groups=mesh['groups'=1,'dp'=16,'mp'=2] {'mp'}, dimensions={1} | all-to-all | bytes 6291456 | tf_op jit(solution)/shard_map/all_to_all | solution.py:43
  275.3 3.3 fusion.32
  278.6 2.3 copy.93
  280.9 2.6 convert_element_type.105
  283.5 4.8 %copy.96 = bf16[64,256,64]{2,1,0:T(8,128)(2,1)} copy(bf16[64,256,64]{1,2,0:T(8,128)(2,1)} %convolution_convert_fusion.2) | data formatting | bytes 4194304 | tf_op jit(solution)/shard_map/convert_element_type | solution.py:117
  288.3 6.5 %convert_element_type.110 = bf16[64,16,1024]{2,1,0:T(8,128)(2,1)} reshape(bf16[64,256,64]{2,1,0:T(8,128)(2,1)} %copy.96) | data formatting | bytes 4194304 | tf_op jit(solution)/shard_map/convert_element_type | solution.py:117
  294.7 3.4 pad_maximum_fusion
  298.1 5.2 %copy.101 = bf16[16,64,2560]{2,1,0:T(8,128)(2,1)} copy(bf16[16,64,2560]{2,0,1:T(8,128)(2,1)S(1)} %pad_maximum_fusion) | data formatting | bytes 10485760 | tf_op jit(solution)/shard_map/concatenate | solution.py:121
  303.3 5.7 %fusion.23 = bf16[64,64,384]{2,1,0:T(8,128)(2,1)} fusion(bf16[64,64,64]{2,1,0:T(8,128)(2,1)} %reshape_reshape.12, bf16[384,64,64]{0,2,1:T(8,128)(2,1)S(1)} %bitcast.105), kind=kOutput, calls=%fused_computation.39 | convolution fusion | flops 202899456 | bytes 6815744 | tf_op jit(solution)/shard_map/tjm,mpj->tmp/dot_general | solution.py:112
  309.0 4.6 %copy.102 = bf16[384,4096]{1,0:T(8,128)(2,1)} copy(bf16[384,4096]{0,1:T(8,128)(2,1)} %bitcast.107) | data formatting | bytes 6291456
  313.6 103.9 %reduce-scatter.2.cloned.1.call-done = bf16[1,64,2560]{2,1,0:T(8,128)(2,1)} async-done(((bf16[16,64,2560]{2,1,0:T(8,128)(2,1)}), bf16[1,64,2560]{2,1,0:T(8,128)(2,1)}) %reduce-scatter.2.cloned.1.call-update) | async-done | bytes 327696 | tf_op jit(solution)/shard_map/reduce_scatter | solution.py:120
  417.6 1.0 bitcast_convert_fusion.1
  419.2 0.8 fusion.40
  (32 shorter events, 2.2 us)
Async XLA Ops:
  7.2 62.2 %all-gather.5.cloned.1.call-start = ((), (), s32[]{:S(2)}) async-start(), calls=%async_computation.6 | async-start | bytes 1114112 | tf_op jit(solution)/shard_map/all_gather | solution.py:57
  8.6 139.0 %all-gather.7.cloned.1.call-start = ((), (), s32[]{:S(2)}) async-start(), calls=%async_computation.7 | async-start | bytes 4456448 | tf_op jit(solution)/shard_map/all_gather | solution.py:57
  10.4 407.1 %reduce-scatter.2.cloned.1.call-start = ((), (), s32[]{:S(2)}) async-start(), calls=%async_computation.5 | async-start | bytes 5570560 | tf_op jit(solution)/shard_map/reduce_scatter | solution.py:120
  13.9 63.0 %copy-start.2 = (bf16[384,4096]{0,1:T(8,128)(2,1)}, bf16[384,4096]{0,1:T(8,128)(2,1)S(1)}, u32[]{:S(2)}) copy-start(bf16[384,4096]{0,1:T(8,128)(2,1)S(1)} %copy.79) | copy-start | bytes 9437188
  13.9 5.4 %copy-start.9 = (s32[1,4]{1,0:T(1,128)S(1)}, s32[1,4]{1,0:T(1,128)}, u32[]{:S(2)}) copy-start(s32[1,4]{1,0:T(1,128)} %param.9) | copy-start | bytes 52
  87.3 3.0 copy-start.4
  87.3 3.3 copy-start.8
  169.0 14.1 %copy-start.1 = (bf16[64,64,256]{2,1,0:T(8,128)(2,1)S(1)}, bf16[64,64,256]{2,1,0:T(8,128)(2,1)}, u32[]{:S(2)}) copy-start(bf16[64,64,256]{2,1,0:T(8,128)(2,1)} %reshape_reshape.13) | copy-start | bytes 6291460
  169.1 14.1 %copy-start.7 = (bf16[384,32,2,64]{0,3,2,1:T(8,128)(2,1)S(1)}, bf16[384,32,2,64]{0,3,2,1:T(8,128)(2,1)}, u32[]{:S(2)}) copy-start(bf16[384,32,2,64]{0,3,2,1:T(8,128)(2,1)} %copy.82) | copy-start | bytes 9437188
  183.1 28.8 %copy-start = (bf16[64,256,64]{2,1,0:T(8,128)(2,1)S(1)}, bf16[64,256,64]{2,1,0:T(8,128)(2,1)}, u32[]{:S(2)}) copy-start(bf16[64,256,64]{2,1,0:T(8,128)(2,1)} %reshape_reshape.14) | copy-start | bytes 6291460
  240.9 7.2 %copy-start.6 = (bf16[64,64,384]{2,1,0:T(8,128)(2,1)S(1)}, bf16[64,64,384]{2,1,0:T(8,128)(2,1)}, u32[]{:S(2)}) copy-start(bf16[64,64,384]{2,1,0:T(8,128)(2,1)} %convolution_convert_fusion) | copy-start | bytes 9437188
  254.5 7.8 %copy-start.5 = (bf16[384,4096]{0,1:T(8,128)(2,1)S(1)}, bf16[384,4096]{0,1:T(8,128)(2,1)}, u32[]{:S(2)}) copy-start(bf16[384,4096]{0,1:T(8,128)(2,1)} %multiply_convert_fusion) | copy-start | bytes 9437188
  268.5 6.8 %copy-start.3 = (bf16[384,4096]{0,1:T(8,128)(2,1)S(1)}, bf16[384,4096]{0,1:T(8,128)(2,1)}, u32[]{:S(2)}) copy-start(bf16[384,4096]{0,1:T(8,128)(2,1)} %copy-done.2) | copy-start | bytes 9437188
Sparse Core Ops, SparseCore 0:
  11.3 57.9 all-gather.4
  72.7 74.8 all-gather.6
  303.4 114.0 reduce-scatter.1

commit v3 on v2

v3 whole, which is shorter than its diff:
```python
import jax
import jax.numpy as jnp
from jax import lax
from jax.experimental import pallas as pl
from jax.experimental.pallas import tpu as pltpu
from jax.sharding import PartitionSpec as P

P_SIZE = 64
Q = 256
SEG_MOST = 96


ROOT = 0.7978845608028654
CUBIC = 0.044715


def token_scale(seg_lengths, count):
    order = jnp.arange(seg_lengths.shape[0], dtype=jnp.int32)
    ends = jnp.sum(
        jnp.where(order[None, :] <= order[:, None], seg_lengths[None, :], 0), axis=1
    )
    starts = ends - seg_lengths
    positions = jnp.arange(count, dtype=jnp.int32)[:, None]
    inside = (positions >= starts[None, :]) & (positions < ends[None, :])
    weights = SEG_MOST / seg_lengths.astype(jnp.float32)
    return jnp.sum(jnp.where(inside, weights[None, :], jnp.zeros_like(weights)[None, :]), axis=1)


def exchange(field, shares):
    field = field.reshape(shares, -1, *field.shape[1:])
    return lax.all_to_all(field, "mp", split_axis=0, concat_axis=0, tiled=True)


def exchange_back(field):
    moved = lax.all_to_all(field, "mp", split_axis=0, concat_axis=0, tiled=True)
    return moved.reshape(-1, *moved.shape[2:])


def middle(mixed_ref, grad_ref, two_ref, three_ref, narrow_ref, d_mixed_ref, g_two_ref, g_three_ref):
    dims = (((1,), (0,)), ((), ()))
    across = (((1,), (1,)), ((), ()))

    def dot(left, right, how=dims):
        return lax.dot_general(left, right, how, preferred_element_type=jnp.float32)

    for h in range(mixed_ref.shape[0]):
        mixed, grad = mixed_ref[h, 0], grad_ref[h, 0]
        two, three = two_ref[h], three_ref[h]
        pre = dot(two.T, mixed)
        square = pre * pre
        wave = jnp.tanh(pre * (ROOT + (ROOT * CUBIC) * square))
        half = 0.5 + 0.5 * wave
        act = (pre * half).astype(jnp.bfloat16)
        narrow_ref[h, 0] = dot(three.T, act).astype(jnp.bfloat16)
        g_three_ref[h] = dot(act, grad, across).astype(jnp.bfloat16)
        slope = half + (pre * (ROOT + (3.0 * ROOT * CUBIC) * square)) * (0.5 - 0.5 * wave * wave)
        d_pre = (slope * dot(three, grad)).astype(jnp.bfloat16)
        d_mixed_ref[h, 0] = dot(two, d_pre).astype(jnp.bfloat16)
        g_two_ref[h] = dot(mixed, d_pre, across).astype(jnp.bfloat16)


def middle_call(mixed, grad, two, three):
    shares, steps, inner, tokens = mixed.shape
    token_spec = pl.BlockSpec((shares, 1, inner, tokens), lambda j: (0, j, 0, 0))

    def weight_spec(array):
        return pl.BlockSpec((shares, *array.shape[1:]), lambda j: (j, 0, 0))

    return pl.pallas_call(
        middle,
        grid=(steps,),
        in_specs=[token_spec, token_spec, weight_spec(two), weight_spec(three)],
        out_specs=[token_spec, token_spec, weight_spec(two), weight_spec(three)],
        out_shape=[
            jax.ShapeDtypeStruct(array.shape, jnp.bfloat16) for array in (mixed, grad, two, three)
        ],
        compiler_params=pltpu.CompilerParams(vmem_limit_bytes=32 * 2**20),
        cost_estimate=pl.CostEstimate(
            flops=12 * two.size * tokens,
            bytes_accessed=4 * (mixed.size + grad.size + two.size + three.size),
            transcendentals=two.size // inner * tokens,
        ),
    )(mixed, grad, two, three)


def shards(tokens, cotangent, lengths, up_first, up_second, down_first, down_second):
    single_float = jnp.float32
    brain_float_half = jnp.bfloat16
    shares = lax.axis_size("mp")
    local_blocks = up_first.shape[0]
    row_count = tokens.shape[0]
    parts = lax.axis_size("dp")

    factors = (up_first, up_second, down_first, down_second)
    whole = lax.all_gather(jnp.concatenate(factors, axis=1), "dp", axis=0)
    unpacked, at = [], 0
    for factor in factors:
        piece = whole[:, :, at : at + factor.shape[1]]
        unpacked.append(piece.transpose(1, 0, 2).reshape(local_blocks, -1))
        at += factor.shape[1]
    whole_one, whole_two, whole_three, whole_four = unpacked
    wone = whole_one.reshape(local_blocks, P_SIZE, P_SIZE)
    wtwo = whole_two.reshape(local_blocks, P_SIZE, Q)
    third_weight = whole_three.reshape(local_blocks, Q, P_SIZE)
    wfour = whole_four.reshape(local_blocks, P_SIZE, P_SIZE)
    blocked = tokens.reshape(row_count, local_blocks, P_SIZE)
    first = jnp.einsum("tmp,mpj->jmt", blocked, wone, preferred_element_type=single_float).astype(
        brain_float_half
    )
    mixed_in = exchange(first, shares)
    scale = token_scale(lengths[0], row_count)
    out_grad = (
        (cotangent.astype(single_float) * scale[:, None])
        .astype(brain_float_half)
        .reshape(row_count, local_blocks, P_SIZE)
    )
    d_mixed_out = jnp.einsum(
        "tmq,mjq->jmt", out_grad, wfour, preferred_element_type=single_float
    ).astype(brain_float_half)
    narrow_gradient = exchange(d_mixed_out, shares)
    narrow, d_mixed_in, g_two, g_three = middle_call(mixed_in, narrow_gradient, wtwo, third_weight)
    mixed_out = exchange_back(narrow)
    d_first = exchange_back(d_mixed_in)
    g_four = jnp.einsum("jmt,tmq->mjq", mixed_out, out_grad, preferred_element_type=single_float)
    g_one = jnp.einsum("tmp,jmt->mpj", blocked, d_first, preferred_element_type=single_float)
    input_grad = jnp.einsum(
        "jmt,mpj->tmp", d_first, wone, preferred_element_type=single_float
    ).astype(brain_float_half)
    input_grad = input_grad.reshape(row_count, local_blocks * P_SIZE)
    pieces = [
        piece.astype(brain_float_half).reshape(local_blocks, parts, -1).transpose(1, 0, 2)
        for piece in (g_one, g_two, g_three, g_four)
    ]
    summed = lax.psum_scatter(
        jnp.concatenate(pieces, axis=2), "dp", scatter_dimension=0, tiled=False
    ).astype(single_float)
    cuts, at = [], 0
    for piece in pieces:
        cuts.append(summed[:, at : at + piece.shape[2]])
        at += piece.shape[2]
    g_one, g_two, g_three, g_four = cuts
    return (input_grad, g_one, g_two, g_three, g_four)


def solution(mesh):
    in_specs = (
        P(("groups", "dp"), "mp"),
        P(("groups", "dp"), "mp"),
        P(("groups", "dp"), None),
        P("mp", "dp"),
        P("mp", "dp"),
        P("mp", "dp"),
        P("mp", "dp"),
    )
    out_specs = (
        P(("groups", "dp"), "mp"),
        P(("groups", "mp"), "dp"),
        P(("groups", "mp"), "dp"),
        P(("groups", "mp"), "dp"),
        P(("groups", "mp"), "dp"),
    )
    return jax.shard_map(shards, mesh=mesh, in_specs=in_specs, out_specs=out_specs, check_vma=False)
```

time: 436 us -> 364 us (0.83); the launches traced: 427 us -> 363 us
  matrix products: 94.4 us -> 17.6 us
  Pallas kernels: 0 us -> 40.5 us
  waiting for transfers between devices: 197 us -> 178 us
  blocking collectives: 27.3 us -> 21 us
  local copies, waits for them, and re-layouts: 82.2 us -> 77.5 us
    dot_general x11 -> x5, matrix products: 94.4 us -> 17.6 us  [the longest x1 5.71 us: shards(): jnp.einsum('jmt,mpj->tmp', d_first, wone, preferred_element_type=single_f...]
    pallas_call x0 -> x1, Pallas kernels: none -> 40.5 us  [middle_call(): pl.pallas_call(middle, grid=(steps,), in_specs=[token_spec, token_spec, w...]
    convert_element_type x6 -> x1, local copies, waits for them, and re-layouts: 23.2 us -> 2.42 us  [shards(): piece.astype(brain_float_half).reshape(local_blocks, parts, -1)]
    all_gather x2 -> x1, waiting for transfers between devices: 92.9 us -> 76.4 us  [shards(): whole = lax.all_gather(jnp.concatenate(factors, axis=1), 'dp', axis=0)]
    reshape x2 -> x4, local copies, waits for them, and re-layouts: 2.42 us -> 12.6 us  [shards(): piece.astype(brain_float_half).reshape(local_blocks, parts, -1)]
    all_to_all x4 -> x3, blocking collectives: 27.3 us -> 21 us  [the longest x2 13.3 us: exchange_back(): moved = lax.all_to_all(field, 'mp', split_axis=0, concat_axis=0, tiled=True)]
    unnamed x25 -> x29, local copies, waits for them, and re-layouts: 21.2 us -> 18.8 us
  transfers between devices with their start and end apart: 3 -> 3, of which waited for: 3 -> 2; matrix products, arithmetic and copies ran while one was open for 10% -> 8% of each run, Pallas kernels for 0% -> 0%
where the time goes in v3:
time: 364 us; the launch traced here: 363 us
  waiting for transfers between devices  178 us (49%)
  local copies, waits for them, and re-layouts  77.5 us (21%)
  Pallas kernels  40.5 us (11%)
  blocking collectives  21 us (6%)
  matrix products  17.6 us (5%)
  between operations  14.2 us (4%)
  other arithmetic  9.91 us (3%)
  starting transfers between devices  4.21 us (1%)
    reduce_scatter x1, waiting for transfers between devices, shards(): lax.psum_scatter(jnp.concatenate(pieces, axis=2), 'dp', scatter_dimension...  102 us
    all_gather x1, waiting for transfers between devices, shards(): whole = lax.all_gather(jnp.concatenate(factors, axis=1), 'dp', axis=0)  76.4 us
    pallas_call x1, Pallas kernels, middle_call(): pl.pallas_call(middle, grid=(steps,), in_specs=[token_spec, token_spec, w...  40.5 us
    unnamed x29, local copies, waits for them, and re-layouts  18.8 us
    all_to_all x2, blocking collectives, exchange_back(): moved = lax.all_to_all(field, 'mp', split_axis=0, concat_axis=0, tiled=True)  13.3 us
    reshape x4, local copies, waits for them, and re-layouts, shards(): piece.astype(brain_float_half).reshape(local_blocks, parts, -1)  12.6 us
    transpose x2, local copies, waits for them, and re-layouts, shards(): unpacked.append(piece.transpose(1, 0, 2).reshape(local_blocks, -1))  8.03 us
    all_to_all x1, blocking collectives, exchange(): return lax.all_to_all(field, 'mp', split_axis=0, concat_axis=0, tiled=True)  7.68 us
  transfers between devices with their start and end apart: 3, of which 2 were waited for; matrix products, arithmetic and copies ran while one was open for 8% of the time, Pallas kernels for 0%

profile of v3, /device:TPU:0, one launch (start us, length us, event | category | flops | bytes accessed | tf_op | source)
XLA Modules:
  0.0 363.2 jit_solution(18312656479960541002)
XLA Ops:
  7.2 0.0 all-gather.3.cloned.1.call-start
  7.2 1.7 pad_maximum_fusion.1
  8.9 0.0 all-gather.3.cloned.1.call-update
  9.0 3.4 copy.59
  12.4 0.0 copy-start.12
  12.4 5.4 %copy.63 = bf16[384,4096]{0,1:T(8,128)(2,1)} copy(bf16[384,4096]{1,0:T(8,128)(2,1)} %param.8) | data formatting | bytes 6291456 | tf_op args[1]
  17.9 0.1 select_reduce_fusion.1
  18.0 0.1 select_reduce_fusion
  18.1 4.2 %multiply_convert_fusion = bf16[384,4096]{0,1:T(8,128)(2,1)} fusion(bf16[384,4096]{0,1:T(8,128)(2,1)} %copy.63, f32[384]{0:T(512)S(1)} %select_reduce_fusion), kind=kLoop, calls=%fused_computation | loop fusion | flops 4718592 | bytes 6292992 | tf_op jit(solution)/shard_map/convert_element_type | solution.py:114
  22.3 76.4 %all-gather.3.cloned.1.call-done = bf16[1024,2560]{1,0:T(8,128)(2,1)} async-done(((bf16[64,2560]{1,0:T(8,128)(2,1)}), bf16[1024,2560]{1,0:T(8,128)(2,1)}) %all-gather.3.cloned.1.call-update) | async-done | bytes 5242896 | tf_op jit(solution)/shard_map/all_gather | solution.py:95
  98.7 1.3 fusion.21
  100.0 5.1 %fusion.20 = (bf16[16,64,1024]{2,1,0:T(8,128)(2,1)}, bf16[16,64,1024]{2,1,0:T(8,128)(2,1)}) fusion(bf16[16,64,2560]{2,1,0:T(8,128)(2,1)} %bitcast.59), kind=kLoop, calls=%fused_computation.29 | loop fusion | bytes 8388608 | tf_op jit(solution)/shard_map/slice | solution.py:98
  105.1 1.6 copy_bitcast_fusion.2
  106.6 2.4 reshape_reshape.13
  109.0 2.4 reshape_reshape.12
  111.4 6.5 %copy_bitcast_fusion = (bf16[64,16,1024]{2,1,0:T(8,128)(2,1)}, bf16[64,16,1024]{2,1,0:T(8,128)(2,1)}) fusion(bf16[16,64,1024]{2,1,0:T(8,128)(2,1)} %get-tuple-element.33, bf16[16,64,1024]{2,1,0:T(8,128)(2,1)} %get-tuple-element.34), kind=kLoop, calls=%fused_computation.11 | loop fusion | bytes 8388608 | tf_op jit(solution)/shard_map/transpose | solution.py:99
  117.8 6.4 %reshape_reshape.15.three_ref = bf16[64,256,64]{2,1,0:T(8,128)(2,1)} reshape(bf16[64,16,1024]{2,1,0:T(8,128)(2,1)} %get-tuple-element.43) | data formatting | bytes 4194304 | tf_op jit(solution)/shard_map/reshape;reshape | solution.py:104
  124.2 4.4 %reshape_reshape.14.two_ref = bf16[64,64,256]{2,1,0:T(8,128)(2,1)} reshape(bf16[64,16,1024]{2,1,0:T(8,128)(2,1)} %get-tuple-element.44) | data formatting | bytes 4194304 | tf_op jit(solution)/shard_map/reshape;reshape | solution.py:103
  128.6 2.2 convert_bitcast_fusion.1
  130.8 3.5 copy.61
  134.3 3.9 %all-to-all-start = ((bf16[2,32,64,384]{3,2,1,0:T(8,128)(2,1)}), bf16[2,32,64,384]{3,2,1,0:T(8,128)(2,1)S(1)}, u32[]{:S(2)}, u32[]{:S(2)}) async-start(bf16[2,32,64,384]{3,2,1,0:T(8,128)(2,1)} %bitcast.54), calls=%async_computation | async-start | bytes 6291456 | tf_op jit(solution)/shard_map/all_to_all | solution.py:31
  138.3 0.2 reduce-scatter.2.cloned.1.call-start
  138.5 3.2 convert_bitcast_fusion
  141.7 3.6 copy.64
  145.3 0.0 all-to-all-done.mixed_ref
  145.3 7.7 %all_to_all.20.grad_ref = bf16[2,32,64,384]{3,2,1,0:T(8,128)(2,1)S(1)} all-to-all(bf16[2,32,64,384]{3,2,1,0:T(8,128)(2,1)} %bitcast.55), channel_id=1, replica_groups=mesh['groups'=1,'dp'=16,'mp'=2] {'mp'}, dimensions={0} | all-to-all | bytes 6291456 | tf_op jit(solution)/shard_map/all_to_all | solution.py:31
  153.0 40.5 %shard_map.110 = (bf16[2,32,64,384]{3,2,1,0:T(8,128)(2,1)S(1)}, bf16[2,32,64,384]{3,2,1,0:T(8,128)(2,1)S(1)}, bf16[64,64,256]{2,1,0:T(8,128)(2,1)S(1)}, bf16[64,256,64]{2,1,0:T(8,128)(2,1)S(1)}) custom-call(bf16[2,32,64,384]{3,2,1,0:T(8,128)(2,1)S(1)} %all-to-all-done.mixed_ref, bf16[2,32,64,384]{3,2,1,0:T(8,128)(2,1)S(1)} %all_to_all.20.grad_ref, ...), custom_call_target="tpu_custom_call" | custom-call | flops 4831838208 | bytes 20971520 | tf_op jit(solution)/shard_map/pallas_call | solution.py:69
  193.5 1.7 copy-done.1
  195.2 6.8 %all_to_all.21 = bf16[2,32,64,384]{3,2,1,0:T(8,128)(2,1)S(1)} all-to-all(bf16[2,32,64,384]{3,2,1,0:T(8,128)(2,1)S(1)} %get-tuple-element.9), channel_id=1, replica_groups=mesh['groups'=1,'dp'=16,'mp'=2] {'mp'}, dimensions={0} | all-to-all | bytes 6291456 | tf_op jit(solution)/shard_map/all_to_all | solution.py:35
  202.0 1.7 copy-done.9
  203.7 3.2 fusion.15
  206.9 2.4 copy.69
  209.3 2.6 reshape.54
  211.9 6.5 %all_to_all.22 = bf16[2,32,64,384]{3,2,1,0:T(8,128)(2,1)S(1)} all-to-all(bf16[2,32,64,384]{3,2,1,0:T(8,128)(2,1)S(1)} %copy-done.2), channel_id=1, replica_groups=mesh['groups'=1,'dp'=16,'mp'=2] {'mp'}, dimensions={0} | all-to-all | bytes 6291456 | tf_op jit(solution)/shard_map/all_to_all | solution.py:35
  218.4 3.2 fusion.12
  221.7 1.9 reshape.58
  223.6 2.6 reshape.55
  226.2 5.5 %reshape.56 = bf16[64,16,1024]{2,1,0:T(8,128)(2,1)S(1)} reshape(bf16[64,256,64]{2,1,0:T(8,128)(2,1)} %copy-done) | data formatting | bytes 4194304 | tf_op jit(solution)/shard_map/reshape | solution.py:131
  231.7 2.8 pad_maximum_fusion
  234.5 5.2 %copy.71 = bf16[16,64,2560]{2,1,0:T(8,128)(2,1)} copy(bf16[16,64,2560]{2,0,1:T(8,128)(2,1)S(1)} %pad_maximum_fusion) | data formatting | bytes 10485760 | tf_op jit(solution)/shard_map/concatenate | solution.py:135
  239.7 0.0 reduce-scatter.2.cloned.1.call-update
  239.7 1.9 copy-done.10
  241.6 5.7 %fusion.6 = bf16[64,64,384]{2,1,0:T(8,128)(2,1)} fusion(bf16[64,64,64]{2,1,0:T(8,128)(2,1)} %reshape_reshape.12, bf16[64,64,384]{2,1,0:T(8,128)(2,1)S(1)} %bitcast.52), kind=kOutput, calls=%fused_computation.10 | convolution fusion | flops 202899456 | bytes 6815744 | tf_op jit(solution)/shard_map/jmt,mpj->tmp/dot_general | solution.py:126
  247.3 4.6 %copy.72 = bf16[384,4096]{1,0:T(8,128)(2,1)} copy(bf16[384,4096]{0,1:T(8,128)(2,1)} %bitcast.53) | data formatting | bytes 6291456
  251.9 102.0 %reduce-scatter.2.cloned.1.call-done = bf16[1,64,2560]{2,1,0:T(8,128)(2,1)} async-done(((bf16[16,64,2560]{2,1,0:T(8,128)(2,1)}), bf16[1,64,2560]{2,1,0:T(8,128)(2,1)}) %reduce-scatter.2.cloned.1.call-update) | async-done | bytes 327696 | tf_op jit(solution)/shard_map/reduce_scatter | solution.py:134
  353.9 1.0 bitcast_convert_fusion
  354.9 0.7 fusion.22
  355.6 0.8 fusion.23
  (24 shorter events, 0.0 us)
Async XLA Ops:
  7.2 91.5 %all-gather.3.cloned.1.call-start = ((), (), s32[]{:S(2)}) async-start(), calls=%async_computation.6 | async-start | bytes 5570560 | tf_op jit(solution)/shard_map/all_gather | solution.py:95
  12.4 116.2 %copy-start.6 = (bf16[384,4096]{0,1:T(8,128)(2,1)}, bf16[384,4096]{0,1:T(8,128)(2,1)S(1)}, u32[]{:S(2)}) copy-start(bf16[384,4096]{0,1:T(8,128)(2,1)S(1)} %copy.59) | copy-start | bytes 9437188
  12.4 5.4 %copy-start.12 = (s32[1,4]{1,0:T(1,128)S(1)}, s32[1,4]{1,0:T(1,128)}, u32[]{:S(2)}) copy-start(s32[1,4]{1,0:T(1,128)} %param.9) | copy-start | bytes 52
  134.3 11.0 %all-to-all-start = ((bf16[2,32,64,384]{3,2,1,0:T(8,128)(2,1)}), bf16[2,32,64,384]{3,2,1,0:T(8,128)(2,1)S(1)}, u32[]{:S(2)}, u32[]{:S(2)}) async-start(bf16[2,32,64,384]{3,2,1,0:T(8,128)(2,1)} %bitcast.54), calls=%async_computation | async-start | bytes 6291456 | tf_op jit(solution)/shard_map/all_to_all | solution.py:31
  138.3 215.6 %reduce-scatter.2.cloned.1.call-start = ((), (), s32[]{:S(2)}) async-start(), calls=%async_computation.5 | async-start | bytes 5570560 | tf_op jit(solution)/shard_map/reduce_scatter | solution.py:134
  145.3 7.7 %copy-start.3 = (bf16[64,64,256]{2,1,0:T(8,128)(2,1)S(1)}, bf16[64,64,256]{2,1,0:T(8,128)(2,1)}, u32[]{:S(2)}) copy-start(bf16[64,64,256]{2,1,0:T(8,128)(2,1)} %reshape_reshape.14.two_ref) | copy-start | bytes 6291460
  193.5 1.7 copy-start.1
  195.2 6.8 %copy-start = (bf16[64,256,64]{2,1,0:T(8,128)(2,1)}, bf16[64,256,64]{2,1,0:T(8,128)(2,1)S(1)}, u32[]{:S(2)}) copy-start(bf16[64,256,64]{2,1,0:T(8,128)(2,1)S(1)} %get-tuple-element.11) | copy-start | bytes 6291460
  195.2 6.8 %copy-start.4 = (bf16[64,64,256]{2,1,0:T(8,128)(2,1)}, bf16[64,64,256]{2,1,0:T(8,128)(2,1)S(1)}, u32[]{:S(2)}) copy-start(bf16[64,64,256]{2,1,0:T(8,128)(2,1)S(1)} %get-tuple-element.10) | copy-start | bytes 6291460
  195.2 8.5 %copy-start.7 = (bf16[384,4096]{0,1:T(8,128)(2,1)S(1)}, bf16[384,4096]{0,1:T(8,128)(2,1)}, u32[]{:S(2)}) copy-start(bf16[384,4096]{0,1:T(8,128)(2,1)} %copy-done.6) | copy-start | bytes 9437188
  202.0 1.7 copy-start.9
  206.9 5.0 %copy-start.2 = (bf16[2,32,64,384]{3,2,1,0:T(8,128)(2,1)S(1)}, bf16[2,32,64,384]{3,2,1,0:T(8,128)(2,1)}, u32[]{:S(2)}) copy-start(bf16[2,32,64,384]{3,2,1,0:T(8,128)(2,1)} %copy-done.1) | copy-start | bytes 9437188
  211.9 6.5 %copy-start.8 = (bf16[384,4096]{0,1:T(8,128)(2,1)S(1)}, bf16[384,4096]{0,1:T(8,128)(2,1)}, u32[]{:S(2)}) copy-start(bf16[384,4096]{0,1:T(8,128)(2,1)} %multiply_convert_fusion) | copy-start | bytes 9437188
  218.4 5.2 %copy-start.5 = (bf16[64,64,256]{2,1,0:T(8,128)(2,1)S(1)}, bf16[64,64,256]{2,1,0:T(8,128)(2,1)}, u32[]{:S(2)}) copy-start(bf16[64,64,256]{2,1,0:T(8,128)(2,1)} %copy-done.4) | copy-start | bytes 6291460
  226.2 5.5 %copy-start.11 = (bf16[64,16,256]{2,1,0:T(8,128)(2,1)S(1)}, bf16[64,16,256]{2,1,0:T(8,128)(2,1)}, u32[]{:S(2)}) copy-start(bf16[64,16,256]{2,1,0:T(8,128)(2,1)} %reshape.54) | copy-start | bytes 1572868
  239.7 1.9 copy-start.10
Sparse Core Ops, SparseCore 0:
  10.7 87.8 all-gather.2
  239.8 113.9 reduce-scatter.1

commit v4 on v3

--- a/solution.py
+++ b/solution.py
@@ -119,6 +119,18 @@
     ).astype(brain_float_half)
     narrow_gradient = exchange(d_mixed_out, shares)
     narrow, d_mixed_in, g_two, g_three = middle_call(mixed_in, narrow_gradient, wtwo, third_weight)
+
+    def packed(*gradients):
+        pieces = [
+            piece.astype(brain_float_half).reshape(local_blocks, parts, -1).transpose(1, 0, 2)
+            for piece in gradients
+        ]
+        return jnp.concatenate(pieces, axis=2)
+
+    large, narrow, d_mixed_in = lax.optimization_barrier(
+        (packed(g_two, g_three), narrow, d_mixed_in)
+    )
+    large = lax.psum_scatter(large, "dp", scatter_dimension=0, tiled=False)
     mixed_out = exchange_back(narrow)
     d_first = exchange_back(d_mixed_in)
     g_four = jnp.einsum("jmt,tmq->mjq", mixed_out, out_grad, preferred_element_type=single_float)
@@ -127,18 +139,10 @@
         "jmt,mpj->tmp", d_first, wone, preferred_element_type=single_float
     ).astype(brain_float_half)
     input_grad = input_grad.reshape(row_count, local_blocks * P_SIZE)
-    pieces = [
-        piece.astype(brain_float_half).reshape(local_blocks, parts, -1).transpose(1, 0, 2)
-        for piece in (g_one, g_two, g_three, g_four)
-    ]
-    summed = lax.psum_scatter(
-        jnp.concatenate(pieces, axis=2), "dp", scatter_dimension=0, tiled=False
-    ).astype(single_float)
-    cuts, at = [], 0
-    for piece in pieces:
-        cuts.append(summed[:, at : at + piece.shape[2]])
-        at += piece.shape[2]
-    g_one, g_two, g_three, g_four = cuts
+    small = lax.all_to_all(packed(g_one, g_four), "dp", split_axis=0, concat_axis=0, tiled=True)
+    small = jnp.sum(small.astype(single_float), axis=0)
+    g_one, g_four = jnp.split(small, 2, axis=1)
+    g_two, g_three = jnp.split(large.astype(single_float), 2, axis=1)
     return (input_grad, g_one, g_two, g_three, g_four)
 
 

time: 364 us -> 335 us (0.920)
  waiting for transfers between devices: 178 us -> 136 us
  local copies, waits for them, and re-layouts: 77.5 us -> 83.4 us
  starting transfers between devices: 4.21 us -> 8.54 us
    reduce_scatter x1, waiting for transfers between devices: 102 us -> 37.7 us  [shards(): large = lax.psum_scatter(large, 'dp', scatter_dimension=0, tiled=False)]
    all_to_all x0 -> x1, waiting for transfers between devices: none -> 21.4 us  [shards(): lax.all_to_all(packed(g_one, g_four), 'dp', split_axis=0, concat_axis=0,...]
    all_to_all x0 -> x1, starting transfers between devices: none -> 4.34 us  [shards(): lax.all_to_all(packed(g_one, g_four), 'dp', split_axis=0, concat_axis=0,...]
    optimization_barrier x0 -> x1, local copies, waits for them, and re-layouts: none -> 4.27 us  [shards(): lax.optimization_barrier((packed(g_two, g_three), narrow, d_mixed_in))]
    unnamed x29 -> x27, local copies, waits for them, and re-layouts: 18.8 us -> 21.8 us
  transfers between devices with their start and end apart: 3 -> 4, of which waited for: 2 -> 3; matrix products, arithmetic and copies ran while one was open for 8% -> 14% of each run, Pallas kernels for 0% -> 0%
where the time goes in v4:
time: 335 us; the launch traced here: 334 us
  waiting for transfers between devices  136 us (41%)
  local copies, waits for them, and re-layouts  83.4 us (25%)
  Pallas kernels  40.5 us (12%)
  blocking collectives  22.3 us (7%)
  matrix products  16.7 us (5%)
  between operations  14.2 us (4%)
  other arithmetic  12.7 us (4%)
  starting transfers between devices  8.54 us (3%)
    all_gather x1, waiting for transfers between devices, shards(): whole = lax.all_gather(jnp.concatenate(factors, axis=1), 'dp', axis=0)  76.4 us
    pallas_call x1, Pallas kernels, middle_call(): pl.pallas_call(middle, grid=(steps,), in_specs=[token_spec, token_spec, w...  40.5 us
    reduce_scatter x1, waiting for transfers between devices, shards(): large = lax.psum_scatter(large, 'dp', scatter_dimension=0, tiled=False)  37.7 us
    unnamed x27, local copies, waits for them, and re-layouts  21.8 us
    all_to_all x1, waiting for transfers between devices, shards(): lax.all_to_all(packed(g_one, g_four), 'dp', split_axis=0, concat_axis=0,...  21.4 us
    reshape x4, local copies, waits for them, and re-layouts, packed(): piece.astype(brain_float_half).reshape(local_blocks, parts, -1)  14.9 us
    all_to_all x2, blocking collectives, exchange_back(): moved = lax.all_to_all(field, 'mp', split_axis=0, concat_axis=0, tiled=True)  14.3 us
    transpose x2, local copies, waits for them, and re-layouts, shards(): unpacked.append(piece.transpose(1, 0, 2).reshape(local_blocks, -1))  8.05 us
  transfers between devices with their start and end apart: 4, of which 3 were waited for; matrix products, arithmetic and copies ran while one was open for 14% of the time, Pallas kernels for 0%

profile of v4, /device:TPU:0, one launch (start us, length us, event | category | flops | bytes accessed | tf_op | source)
XLA Modules:
  0.0 333.9 jit_solution(8948593598466410289)
XLA Ops:
  7.2 1.7 pad_maximum_fusion.2
  9.0 3.4 %copy.59 = bf16[384,4096]{0,1:T(8,128)(2,1)S(1)} copy(bf16[384,4096]{1,0:T(8,128)(2,1)} %param.7) | data formatting | bytes 6291456 | tf_op args[0]
  12.4 5.4 %copy.63 = bf16[384,4096]{0,1:T(8,128)(2,1)} copy(bf16[384,4096]{1,0:T(8,128)(2,1)} %param.8) | data formatting | bytes 6291456 | tf_op args[1]
  18.1 4.2 %multiply_convert_fusion = bf16[384,4096]{0,1:T(8,128)(2,1)} fusion(bf16[384,4096]{0,1:T(8,128)(2,1)} %copy.63, f32[384]{0:T(512)S(1)} %select_reduce_fusion), kind=kLoop, calls=%fused_computation | loop fusion | flops 4718592 | bytes 6292992 | tf_op jit(solution)/shard_map/convert_element_type | solution.py:114
  22.2 76.4 %all-gather.3.cloned.1.call-done = bf16[1024,2560]{1,0:T(8,128)(2,1)} async-done(((bf16[64,2560]{1,0:T(8,128)(2,1)}), bf16[1024,2560]{1,0:T(8,128)(2,1)}) %all-gather.3.cloned.1.call-update) | async-done | bytes 5242896 | tf_op jit(solution)/shard_map/all_gather | solution.py:95
  98.7 1.3 fusion.21
  100.0 5.1 %fusion.20 = (bf16[16,64,1024]{2,1,0:T(8,128)(2,1)}, bf16[16,64,1024]{2,1,0:T(8,128)(2,1)}) fusion(bf16[16,64,2560]{2,1,0:T(8,128)(2,1)} %bitcast.59), kind=kLoop, calls=%fused_computation.31 | loop fusion | bytes 8388608 | tf_op jit(solution)/shard_map/slice | solution.py:98
  105.1 1.6 copy_bitcast_fusion.2
  106.6 2.4 reshape_reshape.13
  109.0 2.4 reshape_reshape.12
  111.4 6.5 %copy_bitcast_fusion = (bf16[64,16,1024]{2,1,0:T(8,128)(2,1)}, bf16[64,16,1024]{2,1,0:T(8,128)(2,1)}) fusion(bf16[16,64,1024]{2,1,0:T(8,128)(2,1)} %get-tuple-element.39, bf16[16,64,1024]{2,1,0:T(8,128)(2,1)} %get-tuple-element.40), kind=kLoop, calls=%fused_computation.11 | loop fusion | bytes 8388608 | tf_op jit(solution)/shard_map/transpose | solution.py:99
  117.9 6.4 %reshape_reshape.15.three_ref = bf16[64,256,64]{2,1,0:T(8,128)(2,1)} reshape(bf16[64,16,1024]{2,1,0:T(8,128)(2,1)} %get-tuple-element.49) | data formatting | bytes 4194304 | tf_op jit(solution)/shard_map/reshape;reshape | solution.py:104
  124.2 4.4 %reshape_reshape.14.two_ref = bf16[64,64,256]{2,1,0:T(8,128)(2,1)} reshape(bf16[64,16,1024]{2,1,0:T(8,128)(2,1)} %get-tuple-element.50) | data formatting | bytes 4194304 | tf_op jit(solution)/shard_map/reshape;reshape | solution.py:103
  128.6 2.2 convert_bitcast_fusion.1
  130.9 3.5 %copy.61 = bf16[64,64,384]{2,1,0:T(8,128)(2,1)} copy(bf16[64,64,384]{2,0,1:T(8,128)(2,1)S(1)} %convert_bitcast_fusion.1) | data formatting | bytes 6291456 | tf_op jit(solution)/shard_map/convert_element_type | solution.py:107
  134.4 3.9 %all-to-all-start = ((bf16[2,32,64,384]{3,2,1,0:T(8,128)(2,1)}), bf16[2,32,64,384]{3,2,1,0:T(8,128)(2,1)S(1)}, u32[]{:S(2)}, u32[]{:S(2)}) async-start(bf16[2,32,64,384]{3,2,1,0:T(8,128)(2,1)} %bitcast.54), calls=%async_computation | async-start | bytes 6291456 | tf_op jit(solution)/shard_map/all_to_all | solution.py:31
  138.3 0.2 reduce-scatter.2.cloned.1.call-start
  138.6 3.2 convert_bitcast_fusion
  141.8 3.6 %copy.64 = bf16[64,64,384]{2,1,0:T(8,128)(2,1)} copy(bf16[64,64,384]{2,0,1:T(8,128)(2,1)S(1)} %convert_bitcast_fusion) | data formatting | bytes 6291456 | tf_op jit(solution)/shard_map/convert_element_type | solution.py:119
  145.4 1.7 copy-done.1
  147.0 7.9 %all_to_all.25.grad_ref = bf16[2,32,64,384]{3,2,1,0:T(8,128)(2,1)S(1)} all-to-all(bf16[2,32,64,384]{3,2,1,0:T(8,128)(2,1)} %bitcast.55), channel_id=1, replica_groups=mesh['groups'=1,'dp'=16,'mp'=2] {'mp'}, dimensions={0} | all-to-all | bytes 6291456 | tf_op jit(solution)/shard_map/all_to_all | solution.py:31
  155.0 40.5 %shard_map.110 = (bf16[2,32,64,384]{3,2,1,0:T(8,128)(2,1)S(1)}, bf16[2,32,64,384]{3,2,1,0:T(8,128)(2,1)S(1)}, bf16[64,64,256]{2,1,0:T(8,128)(2,1)S(1)}, bf16[64,256,64]{2,1,0:T(8,128)(2,1)S(1)}) custom-call(bf16[2,32,64,384]{3,2,1,0:T(8,128)(2,1)S(1)} %copy-done.2, bf16[2,32,64,384]{3,2,1,0:T(8,128)(2,1)S(1)} %all_to_all.25.grad_ref, ...), custom_call_target="tpu_custom_call" | custom-call | flops 4831838208 | bytes 20971520 | tf_op jit(solution)/shard_map/pallas_call | solution.py:69
  195.5 2.0 copy-done
  197.4 1.7 copy-done.3
  199.1 1.3 copy-done.5
  200.4 4.4 %reshape.52 = bf16[64,16,1024]{2,1,0:T(8,128)(2,1)} reshape(bf16[64,64,256]{2,1,0:T(8,128)(2,1)} %copy-done.5) | data formatting | bytes 4194304 | tf_op jit(solution)/shard_map/reshape | solution.py:125
  204.8 6.5 %reshape.53 = bf16[64,16,1024]{2,1,0:T(8,128)(2,1)} reshape(bf16[64,256,64]{2,1,0:T(8,128)(2,1)} %copy-done) | data formatting | bytes 4194304 | tf_op jit(solution)/shard_map/reshape | solution.py:125
  211.3 2.8 pad_maximum_fusion
  214.1 4.3 %copy.72 = bf16[16,64,2048]{2,1,0:T(8,128)(2,1)} copy(bf16[16,64,2048]{2,0,1:T(8,128)(2,1)S(1)} %pad_maximum_fusion) | data formatting | bytes 8388608 | tf_op jit(solution)/shard_map/optimization_barrier | solution.py:130
  218.4 7.8 %all_to_all.26 = bf16[2,32,64,384]{3,2,1,0:T(8,128)(2,1)S(1)} all-to-all(bf16[2,32,64,384]{3,2,1,0:T(8,128)(2,1)} %copy-done.3), channel_id=1, replica_groups=mesh['groups'=1,'dp'=16,'mp'=2] {'mp'}, dimensions={0} | all-to-all | bytes 6291456 | tf_op jit(solution)/shard_map/all_to_all | solution.py:35
  226.2 1.7 copy-done.9
  227.9 3.3 fusion.15
  231.1 2.3 copy.69
  233.4 2.6 reshape.56
  236.0 6.5 %all_to_all.27 = bf16[2,32,64,384]{3,2,1,0:T(8,128)(2,1)S(1)} all-to-all(bf16[2,32,64,384]{3,2,1,0:T(8,128)(2,1)S(1)} %get-tuple-element.17), channel_id=1, replica_groups=mesh['groups'=1,'dp'=16,'mp'=2] {'mp'}, dimensions={0} | all-to-all | bytes 6291456 | tf_op jit(solution)/shard_map/all_to_all | solution.py:35
  242.6 2.2 fusion.12
  244.8 1.5 reshape.58
  246.3 1.5 pad_maximum_fusion.1
  247.7 1.6 copy.71
  249.4 4.3 %all-to-all-start.4 = ((bf16[16,64,512]{2,1,0:T(8,128)(2,1)}), bf16[16,64,512]{2,1,0:T(8,128)(2,1)}, u32[]{:S(2)}, u32[]{:S(2)}) async-start(bf16[16,64,512]{2,1,0:T(8,128)(2,1)} %copy.71), calls=%async_computation.4 | async-start | bytes 2097152 | tf_op jit(solution)/shard_map/all_to_all | solution.py:142
  253.7 5.7 %fusion.6 = bf16[64,64,384]{2,1,0:T(8,128)(2,1)} fusion(bf16[64,64,64]{2,1,0:T(8,128)(2,1)} %reshape_reshape.12, bf16[64,64,384]{2,1,0:T(8,128)(2,1)S(1)} %bitcast.52), kind=kOutput, calls=%fused_computation.10 | convolution fusion | flops 202899456 | bytes 6815744 | tf_op jit(solution)/shard_map/jmt,mpj->tmp/dot_general | solution.py:138
  259.5 4.6 %copy.73 = bf16[384,4096]{1,0:T(8,128)(2,1)} copy(bf16[384,4096]{0,1:T(8,128)(2,1)} %bitcast.53) | data formatting | bytes 6291456
  264.1 21.4 %all-to-all-done.4 = bf16[16,64,512]{2,1,0:T(8,128)(2,1)} async-done(((bf16[16,64,512]{2,1,0:T(8,128)(2,1)}), bf16[16,64,512]{2,1,0:T(8,128)(2,1)}, u32[]{:S(2)}, u32[]{:S(2)}) %all-to-all-start.4) | async-done | bytes 1048608 | tf_op jit(solution)/shard_map/all_to_all | solution.py:142
  285.5 1.4 convert_reduce_fusion
  286.9 0.7 fusion.23
  287.6 37.7 %reduce-scatter.2.cloned.1.call-done = bf16[1,64,2048]{2,1,0:T(8,128)(2,1)} async-done(((bf16[16,64,2048]{2,1,0:T(8,128)(2,1)}), bf16[1,64,2048]{2,1,0:T(8,128)(2,1)}) %reduce-scatter.2.cloned.1.call-update) | async-done | bytes 262160 | tf_op jit(solution)/shard_map/reduce_scatter | solution.py:133
  325.2 1.0 bitcast_convert_fusion
  326.2 0.8 fusion.22
  (27 shorter events, 0.3 us)
Async XLA Ops:
  7.2 91.5 %all-gather.3.cloned.1.call-start = ((), (), s32[]{:S(2)}) async-start(), calls=%async_computation.7 | async-start | bytes 5570560 | tf_op jit(solution)/shard_map/all_gather | solution.py:95
  12.4 116.2 %copy-start.6 = (bf16[384,4096]{0,1:T(8,128)(2,1)}, bf16[384,4096]{0,1:T(8,128)(2,1)S(1)}, u32[]{:S(2)}) copy-start(bf16[384,4096]{0,1:T(8,128)(2,1)S(1)} %copy.59) | copy-start | bytes 9437188
  12.4 5.4 %copy-start.11 = (s32[1,4]{1,0:T(1,128)S(1)}, s32[1,4]{1,0:T(1,128)}, u32[]{:S(2)}) copy-start(s32[1,4]{1,0:T(1,128)} %param.9) | copy-start | bytes 52
  134.4 11.0 %all-to-all-start = ((bf16[2,32,64,384]{3,2,1,0:T(8,128)(2,1)}), bf16[2,32,64,384]{3,2,1,0:T(8,128)(2,1)S(1)}, u32[]{:S(2)}, u32[]{:S(2)}) async-start(bf16[2,32,64,384]{3,2,1,0:T(8,128)(2,1)} %bitcast.54), calls=%async_computation | async-start | bytes 6291456 | tf_op jit(solution)/shard_map/all_to_all | solution.py:31
  138.3 186.9 %reduce-scatter.2.cloned.1.call-start = ((), (), s32[]{:S(2)}) async-start(), calls=%async_computation.6 | async-start | bytes 4456448 | tf_op jit(solution)/shard_map/reduce_scatter | solution.py:133
  145.3 1.7 copy-start.1
  147.0 8.0 %copy-start.2 = (bf16[2,32,64,384]{3,2,1,0:T(8,128)(2,1)S(1)}, bf16[2,32,64,384]{3,2,1,0:T(8,128)(2,1)}, u32[]{:S(2)}) copy-start(bf16[2,32,64,384]{3,2,1,0:T(8,128)(2,1)} %copy-done.1) | copy-start | bytes 9437188
  147.0 8.0 %copy-start.4 = (bf16[64,64,256]{2,1,0:T(8,128)(2,1)S(1)}, bf16[64,64,256]{2,1,0:T(8,128)(2,1)}, u32[]{:S(2)}) copy-start(bf16[64,64,256]{2,1,0:T(8,128)(2,1)} %reshape_reshape.14.two_ref) | copy-start | bytes 6291460
  195.5 2.0 copy-start
  197.4 1.7 copy-start.3
  199.1 1.3 copy-start.5
  218.4 9.5 %copy-start.7 = (bf16[384,4096]{0,1:T(8,128)(2,1)S(1)}, bf16[384,4096]{0,1:T(8,128)(2,1)}, u32[]{:S(2)}) copy-start(bf16[384,4096]{0,1:T(8,128)(2,1)} %copy-done.6) | copy-start | bytes 9437188
  226.2 1.7 copy-start.9
  236.0 6.5 %copy-start.8 = (bf16[384,4096]{0,1:T(8,128)(2,1)S(1)}, bf16[384,4096]{0,1:T(8,128)(2,1)}, u32[]{:S(2)}) copy-start(bf16[384,4096]{0,1:T(8,128)(2,1)} %multiply_convert_fusion) | copy-start | bytes 9437188
  246.3 7.5 %copy-start.10 = (bf16[2,32,64,384]{3,2,1,0:T(8,128)(2,1)S(1)}, bf16[2,32,64,384]{3,2,1,0:T(8,128)(2,1)}, u32[]{:S(2)}) copy-start(bf16[2,32,64,384]{3,2,1,0:T(8,128)(2,1)} %copy-done.9) | copy-start | bytes 9437188
  249.4 36.1 %all-to-all-start.4 = ((bf16[16,64,512]{2,1,0:T(8,128)(2,1)}), bf16[16,64,512]{2,1,0:T(8,128)(2,1)}, u32[]{:S(2)}, u32[]{:S(2)}) async-start(bf16[16,64,512]{2,1,0:T(8,128)(2,1)} %copy.71), calls=%async_computation.4 | async-start | bytes 2097152 | tf_op jit(solution)/shard_map/all_to_all | solution.py:142
Sparse Core Ops, SparseCore 0:
  10.7 87.8 all-gather.2
  218.5 106.6 reduce-scatter.1
